TPU v7x, 32 devices: a whole 2x2x4 slice. The times are simulated.
32 devices in a mesh: rep: 8 (over z, x), grp: 4 (over y, core).
Axes of the slice: x: 2, y: 2, z: 4, core: 2. Of those that a mesh axis runs over, the one named last changes fastest.
Arguments:
- tokens: bfloat16 [8, 2048, 768], P('rep', 'grp'), may hold values from -6 to 6
- segment_ids: int32 [8, 2048], P('rep'), may hold values from 0 to 9, as said below
- w_qkv: bfloat16 [768, 2304], P('grp'), may hold values from -0.21875 to 0.21875
- w_out: bfloat16 [768, 768], P('grp'), may hold values from -1.75 to 1.75
- w_up: bfloat16 [768, 3072], P('grp'), may hold values from -0.21875 to 0.21875
- w_down: bfloat16 [3072, 768], P('grp'), may hold values from -0.109375 to 0.109375
- norm_gains: float32 [2, 768], replicated, may hold values from 0.5 to 1.5
- norm_shifts: float32 [2, 768], replicated, may hold values from -1.2 to 1.2
- proj_biases: float32 [4, 768], replicated, may hold values from -1.2 to 1.2
- up_bias: float32 [3072], replicated, may hold values from -1.8 to 1.8
- cotangent: bfloat16 [8, 2048, 768], P('rep', 'grp'), may hold values from -6 to 6
Outputs:
- block_out: bfloat16 [8, 2048, 768], P('rep', 'grp')
- input_grad: float32 [8, 2048, 768], P('rep', 'grp')
- grad_qkv: float32 [768, 2304], P('grp')
- grad_out: float32 [768, 768], P('grp')
- grad_up: float32 [768, 3072], P('grp')
- grad_down: float32 [3072, 768], P('grp')
- grad_gains: float32 [2, 768], replicated
- grad_shifts: float32 [2, 768], replicated
- grad_biases: float32 [4, 768], replicated
- grad_up_bias: float32 [3072], replicated
Inputs may be any that keep to these rules, and one draw needn't show every extreme that they name: `segment_ids`: in each sequence the ids start at 0 and never fall. In one sequence, drawn from the seed, there are three documents and the middle one begins within the first 512 tokens and ends within the last 512; in the others there are ten documents, each but the last of 102 to 204 tokens.
All inputs are finite; a program needn't handle non-finite values.
Results may differ from a plain program's by a relative error of at most 0.017.
Values may be sent and summed in bfloat16 or wider, within the bound.
No kernel may reach another device: no remote copies, remote signals or barrier semaphores. Data moves between devices by JAX's collectives and lax.ppermute only.
A program may use at most 128 MiB of HBM per device.

v0:
```python
import functools
import math

import jax
import jax.numpy as jnp
from jax import lax
from jax.experimental import pallas as pl
from jax.experimental.pallas import tpu as pltpu
from jax.sharding import PartitionSpec as P

D = 768
H = 12
HD = 64
FF = 3072
PAIRS = H // 2
LANES = 2 * HD
NEG = -1e30
SCALE = 1.0 / math.sqrt(HD)
F32 = jnp.float32
BF16 = jnp.bfloat16


def layer_norm(values, gain_row, shift_row):
    centre = values - jnp.mean(values, axis=-1, keepdims=True)
    spread = jnp.mean(centre * centre, axis=-1, keepdims=True)
    return centre * lax.rsqrt(spread + 1e-05) * gain_row + shift_row


def add_rows(left, piece):
    return jnp.dot(left, piece, preferred_element_type=F32)


def back_rows(right, piece):
    return jnp.einsum("te,ce->tc", right, piece, preferred_element_type=F32)


def token_product(left, right):
    return jnp.einsum("tc,te->ce", left, right, preferred_element_type=F32)


def swap(value, axis, size, mask):
    return lax.ppermute(value, axis, [(i, i ^ mask) for i in range(size)])


def bits_of(size):
    return size.bit_length() - 1


def gather_near(value, size):
    blocks = value[None]
    for bit in list(range(1, bits_of(size))) + [0]:
        blocks = jnp.concatenate([blocks, swap(blocks, "grp", size, 1 << bit)], axis=0)
    return blocks


def gather_later(value, size):
    blocks = value[None]
    for bit in list(range(1, bits_of(size))) + [0]:
        mask = 1 << bit
        if bit == 0:
            pairs = [(i, i ^ 1) for i in range(size)]
        else:
            pairs = [(i, i ^ mask) for i in range(size) if i & mask]
        blocks = jnp.concatenate([blocks, lax.ppermute(blocks, "grp", pairs)], axis=0)
    return blocks


def block_place(block, me, size):
    near = block ^ me
    return (near >> 1) | ((near & 1) << (bits_of(size) - 1))


def after(value, *others):
    return lax.optimization_barrier((value,) + others)[0]


def far_rows(weight, rep, size, reps, spread, *others):
    rows = weight.shape[0]
    side = rep & 1
    pieces = [(0, 0, weight)]
    for bit in range(1, bits_of(size)):
        mask = 1 << bit
        found = []
        for near, first, piece in pieces:
            if spread and near == 0:
                half = rows // 2
                part = lax.dynamic_slice_in_dim(piece, side * half, half, 0)
                got = swap(after(part, *others), "grp", size, mask)
                found.append((near | mask, side * half, got))
                found.append((near | mask, (1 - side) * half, swap(got, "rep", reps, 1)))
            else:
                found.append((near | mask, first, swap(after(piece, *others), "grp", size, mask)))
        pieces = pieces + found
    return pieces


def gather_weight(weight, pieces, me, size):
    rows, columns = weight.shape
    whole = jnp.zeros((size * rows, columns), weight.dtype)
    for near, first, piece in pieces:
        other = swap(piece, "grp", size, 1)
        whole = lax.dynamic_update_slice(whole, piece, ((me ^ near) * rows + first, 0))
        whole = lax.dynamic_update_slice(whole, other, ((me ^ near ^ 1) * rows + first, 0))
    return whole


def by_core(left, me, size):
    rows = left.shape[1] // size
    strips = [left[:, i * rows : (i + 1) * rows] for i in range(size)]
    even = jnp.concatenate(strips[0::2], axis=1)
    odd = jnp.concatenate(strips[1::2], axis=1)
    core = me & 1
    return jnp.where(core == 0, odd, even), jnp.where(core == 0, even, odd)


def core_grad(theirs, terms, size):
    got = swap(theirs, "grp", size, 1).astype(F32)
    mine = jnp.concatenate([token_product(left, right) for left, right in terms], axis=1)
    part = (mine + got).astype(BF16)
    return part.reshape(size // 2, -1, part.shape[1])


def other_grad(terms):
    return jnp.concatenate([token_product(left, right).astype(BF16) for left, right in terms], axis=1)


def group_step(part, bit, me, send_more=None):
    size_left, rows, columns = part.shape
    split = part.reshape(2, size_left // 2, rows, columns)
    side = (me >> bit) & 1
    send = lax.dynamic_index_in_dim(split, 1 - side, 0, keepdims=False)
    keep = lax.dynamic_index_in_dim(split, side, 0, keepdims=False)
    return send, keep


def add_low(keep, got):
    return (keep.astype(F32) + got.astype(F32)).astype(BF16)


def spread_grad(part, me, rep, size, reps, early):
    steps = [("rep", bit) for bit in early]
    steps += [("grp", bit) for bit in range(bits_of(size) - 1, 0, -1)]
    steps += [("rep", bit) for bit in range(bits_of(reps)) if bit not in early]
    undo = []
    for axis, bit in steps:
        if axis == "grp":
            send, keep = group_step(part, bit, me)
            part = add_low(keep, swap(send, "grp", size, 1 << bit))
        else:
            side = (rep >> bit) & 1
            half = part.shape[1] // 2
            send = lax.dynamic_slice_in_dim(part, (1 - side) * half, half, 1)
            keep = lax.dynamic_slice_in_dim(part, side * half, half, 1)
            part = add_low(keep, swap(send, "rep", reps, 1 << bit))
            undo.insert(0, bit)
    for bit in undo:
        side = (rep >> bit) & 1
        got = swap(part, "rep", reps, 1 << bit)
        low, high = jnp.where(side == 0, part, got), jnp.where(side == 0, got, part)
        part = jnp.concatenate([low, high], axis=1)
    return part[0].astype(F32)


def halves(vector):
    high = vector.astype(BF16)
    return jnp.concatenate([high, (vector - high.astype(F32)).astype(BF16)], axis=-2)


def from_halves(pair):
    count = pair.shape[-2] // 2
    return pair[..., :count, :].astype(F32) + pair[..., count:, :].astype(F32)


def spread_last(part, vector, me, size, reps):
    columns = part.shape[2]
    vector = vector + swap(vector, "grp", size, 1)
    for bit in range(bits_of(size) - 1, 0, -1):
        send, keep = group_step(part, bit, me)
        count = send.shape[0] * send.shape[1]
        both = jnp.concatenate([send.reshape(count, columns), halves(vector)], axis=0)
        got = swap(both, "grp", size, 1 << bit)
        part = add_low(keep, got[:count].reshape(keep.shape))
        vector = vector + from_halves(got[count:])
    pieces = part[0].reshape(reps, -1, columns)
    count = pieces.shape[1]
    extra = halves(vector)
    extra = jnp.broadcast_to(extra[None], (reps,) + extra.shape)
    got = lax.all_to_all(jnp.concatenate([pieces, extra], axis=1), "rep", 0, 0, tiled=True)
    own = jnp.sum(got[:, :count].astype(F32), axis=0).astype(BF16)
    vector = jnp.sum(from_halves(got[:, count:]), axis=0)
    every = lax.all_to_all(jnp.broadcast_to(own[None], pieces.shape), "rep", 0, 0, tiled=True)
    return every.reshape(-1, columns).astype(F32), vector


def dot_nt(left, right):
    return lax.dot_general(left, right, (((1,), (1,)), ((), ())), preferred_element_type=F32)


def dot_nn(left, right):
    return lax.dot_general(left, right, (((1,), (0,)), ((), ())), preferred_element_type=F32)


def one_head(pair, head):
    lane = lax.broadcasted_iota(jnp.int32, pair.shape, 1)
    inside = (lane < HD) if head == 0 else (lane >= HD)
    return jnp.where(inside, pair, jnp.zeros_like(pair))


def per_head(first, second, shape):
    lane = lax.broadcasted_iota(jnp.int32, shape, 1)
    return jnp.where(lane < HD, first, second)


def start_of(block, me, size, count):
    return pl.multiple_of(block_place(block, me, size) * count, count)


def query_mask(info, qseg, kseg, bias, tile, count):
    me = info[0]
    for q in range(count // tile):
        rows = pl.ds(q * tile, tile)

        def fill(block, _):
            columns = pl.ds(pl.multiple_of(block * count, count), count)
            q_pos = me * count + q * tile + lax.broadcasted_iota(jnp.int32, (tile, count), 0)
            k_pos = block * count + lax.broadcasted_iota(jnp.int32, (tile, count), 1)
            seen = (k_pos <= q_pos) & (qseg[rows, 0:1] == kseg[0:1, columns])
            bias[rows, columns] = jnp.where(seen, 0.0, NEG)
            return 0

        lax.fori_loop(info[1 + q], me + 1, fill, 0)


def attend_kernel(size, tile, info, q_ref, k_ref, v_ref, qseg, kseg, out, out_low, lse, lse_row, bias):
    count = q_ref.shape[0]
    me = info[0]

    @pl.when(pl.program_id(0) == 0)
    def _():
        query_mask(info, qseg, kseg, bias, tile, count)

    for q in range(count // tile):
        rows = pl.ds(q * tile, tile)
        queries = q_ref[rows, :] * jnp.asarray(SCALE, BF16)

        def step(block, carry):
            tops, sums, total = carry
            start = start_of(block, me, size, count)
            keys = k_ref[pl.ds(start, count), :]
            values = v_ref[pl.ds(start, count), :]
            add = bias[rows, pl.ds(pl.multiple_of(block * count, count), count)]
            new_tops, new_sums, shrinks = [], [], []
            gain = jnp.zeros((tile, LANES), F32)
            for head in range(2):
                scores = dot_nt(queries, one_head(keys, head)) + add
                top = jnp.maximum(tops[head], jnp.max(scores, axis=1, keepdims=True))
                weights = jnp.exp(scores - top)
                shrink = jnp.exp(tops[head] - top)
                new_tops.append(top)
                shrinks.append(shrink)
                new_sums.append(sums[head] * shrink + jnp.sum(weights, axis=1, keepdims=True))
                gain = gain + dot_nn(weights.astype(BF16), one_head(values, head))
            total = total * per_head(shrinks[0], shrinks[1], total.shape) + gain
            return (tuple(new_tops), tuple(new_sums), total)

        column = jnp.zeros((tile, 1), F32)
        tops, sums, total = lax.fori_loop(
            info[1 + q],
            me + 1,
            step,
            ((column + NEG, column + NEG), (column, column), jnp.zeros((tile, LANES), F32)),
        )
        shape = (tile, LANES)
        result = total / per_head(sums[0], sums[1], shape)
        log_total = per_head(tops[0] + jnp.log(sums[0]), tops[1] + jnp.log(sums[1]), shape)
        out[rows, :] = result
        out_low[rows, :] = result.astype(BF16)
        lse[rows, :] = log_total
        turned = log_total.T
        lse_row[0, :, rows] = jnp.zeros((8, tile), F32)
        lse_row[0, 0:1, rows] = turned[0:1, :]
        lse_row[0, 1:2, rows] = turned[HD : HD + 1, :]


def query_grad_kernel(size, tile, info, q_ref, k_ref, v_ref, dout, out, lse, qseg, kseg, dq, bias):
    count = q_ref.shape[0]
    me = info[0]

    @pl.when(pl.program_id(0) == 0)
    def _():
        query_mask(info, qseg, kseg, bias, tile, count)

    for q in range(count // tile):
        rows = pl.ds(q * tile, tile)
        queries = q_ref[rows, :] * jnp.asarray(SCALE, BF16)
        douts = dout[rows, :]
        both = douts.astype(F32) * out[rows, :]
        deltas = [jnp.sum(one_head(both, head), axis=1, keepdims=True) for head in range(2)]
        logs = [lse[rows, 0:1], lse[rows, HD : HD + 1]]

        def step(block, total):
            start = start_of(block, me, size, count)
            keys = k_ref[pl.ds(start, count), :]
            values = v_ref[pl.ds(start, count), :]
            add = bias[rows, pl.ds(pl.multiple_of(block * count, count), count)]
            for head in range(2):
                one_keys = one_head(keys, head)
                scores = dot_nt(queries, one_keys) + add
                probs = jnp.exp(scores - logs[head])
                prob_grad = dot_nt(douts, one_head(values, head))
                score_grad = (probs * (prob_grad - deltas[head])).astype(BF16)
                total = total + dot_nn(score_grad, one_keys)
            return total

        total = lax.fori_loop(info[1 + q], me + 1, step, jnp.zeros((tile, LANES), F32))
        dq[rows, :] = (total * SCALE).astype(BF16)


def key_grad_kernel(
    size, tile, info, k_ref, v_ref, q_ref, dout, stats, kseg, qseg, dk, dv, bias
):
    count = k_ref.shape[0]
    me = info[0]
    first = 1 + count // tile

    @pl.when(pl.program_id(0) == 0)
    def _():
        for k in range(count // tile):
            rows = pl.ds(k * tile, tile)

            def fill(block, _):
                columns = pl.ds(pl.multiple_of(block * count, count), count)
                k_pos = me * count + k * tile + lax.broadcasted_iota(jnp.int32, (tile, count), 0)
                q_pos = block * count + lax.broadcasted_iota(jnp.int32, (tile, count), 1)
                seen = (k_pos <= q_pos) & (kseg[rows, 0:1] == qseg[0:1, columns])
                bias[rows, columns] = jnp.where(seen, 0.0, NEG)
                return 0

            lax.fori_loop(me, info[first + k], fill, 0)

    for k in range(count // tile):
        rows = pl.ds(k * tile, tile)
        keys = k_ref[rows, :]
        values = v_ref[rows, :]

        def step(block, carry):
            key_total, value_total = carry
            place = block_place(block, me, size)
            start = pl.multiple_of(place * count, count)
            queries = q_ref[pl.ds(start, count), :] * jnp.asarray(SCALE, BF16)
            douts = dout[pl.ds(start, count), :]
            add = bias[rows, pl.ds(pl.multiple_of(block * count, count), count)]
            for head in range(2):
                one_queries = one_head(queries, head)
                one_douts = one_head(douts, head)
                scores = dot_nt(keys, one_queries) + add
                probs = jnp.exp(scores - stats[place, 0, head : head + 1, :])
                prob_grad = dot_nt(values, one_douts)
                score_grad = probs * (prob_grad - stats[place, 0, 2 + head : 3 + head, :])
                value_total = value_total + dot_nn(probs.astype(BF16), one_douts)
                key_total = key_total + dot_nn(score_grad.astype(BF16), one_queries)
            return (key_total, value_total)

        empty = jnp.zeros((tile, LANES), F32)
        key_total, value_total = lax.fori_loop(me, info[first + k], step, (empty, empty))
        dk[rows, :] = key_total.astype(BF16)
        dv[rows, :] = value_total.astype(BF16)


def strip(rows, first):
    return pl.BlockSpec((rows, LANES), lambda p, info: (0, first + p))


def whole(shape):
    return pl.BlockSpec(shape, lambda p, info: (0,) * len(shape))


def paired(count, blocks, first=0):
    if blocks is None:
        return pl.BlockSpec((1, 8, count), lambda p, info: (p, 0, 0))
    return pl.BlockSpec((blocks, 1, 8, count), lambda p, info: (0, first + p, 0, 0))


def call(body, in_specs, out_specs, out_shape, count, seq_len, products, pairs):
    return pl.pallas_call(
        body,
        grid_spec=pltpu.PrefetchScalarGridSpec(
            num_scalar_prefetch=1,
            grid=(pairs,),
            in_specs=in_specs,
            out_specs=out_specs,
            scratch_shapes=[pltpu.VMEM((count, seq_len), F32)],
        ),
        out_shape=out_shape,
        compiler_params=pltpu.CompilerParams(vmem_limit_bytes=40 * 1024 * 1024),
        cost_estimate=pl.CostEstimate(
            flops=products * 2 * count * count * 2 * 256 * 2 * pairs,
            bytes_accessed=8 * 1024 * 1024,
            transcendentals=count * count * 4 * pairs,
        ),
    )


def attend(info, qkv_all, seg_col, seg_row, count, seq_len, size, tile):
    out = jax.ShapeDtypeStruct((count, D), F32)
    return call(
        functools.partial(attend_kernel, size, tile),
        [strip(count, 0), strip(seq_len, PAIRS), strip(seq_len, 2 * PAIRS), whole((count, 128)), whole((1, seq_len))],
        [strip(count, 0), strip(count, 0), strip(count, 0), paired(count, None)],
        [out, jax.ShapeDtypeStruct((count, D), BF16), out, jax.ShapeDtypeStruct((PAIRS, 8, count), F32)],
        count,
        seq_len,
        2,
        PAIRS,
    )(info, qkv_all, qkv_all, qkv_all, seg_col, seg_row)


def query_grads(first, pairs, info, qkv_all, dout, out, lse, seg_col, seg_row, count, seq_len, size, tile):
    return call(
        functools.partial(query_grad_kernel, size, tile),
        [strip(count, first), strip(seq_len, PAIRS + first), strip(seq_len, 2 * PAIRS + first)]
        + [strip(count, first)] * 3
        + [whole((count, 128)), whole((1, seq_len))],
        strip(count, 0),
        jax.ShapeDtypeStruct((count, pairs * LANES), BF16),
        count,
        seq_len,
        3,
        pairs,
    )(info, qkv_all, qkv_all, qkv_all, dout, out, lse, seg_col, seg_row)


def key_grads(first, pairs, info, qkv_all, dout_all, stats, seg_col, seg_row, count, seq_len, size, tile):
    grad = jax.ShapeDtypeStruct((count, pairs * LANES), BF16)
    return call(
        functools.partial(key_grad_kernel, size, tile),
        [strip(count, PAIRS + first), strip(count, 2 * PAIRS + first), strip(seq_len, first), strip(seq_len, first)]
        + [paired(count, size, first)]
        + [whole((count, 128)), whole((1, seq_len))],
        [strip(count, 0), strip(count, 0)],
        [grad, grad],
        count,
        seq_len,
        4,
        pairs,
    )(info, qkv_all, qkv_all, qkv_all, dout_all, stats, seg_col, seg_row)


def per_device(
    reps,
    size,
    tokens,
    segment_ids,
    w_qkv,
    w_out,
    w_up,
    w_down,
    norm_gains,
    norm_shifts,
    proj_biases,
    up_bias,
    cotangent,
):
    count = tokens.shape[1]
    seq_len = segment_ids.shape[1]
    tile = min(256, count)
    me = lax.axis_index("grp")
    rep = lax.axis_index("rep")
    seg_row = segment_ids[0]
    first_row = me * count
    own_seg = lax.dynamic_slice_in_dim(seg_row, first_row, count, 0)
    seg_col = jnp.broadcast_to(own_seg[:, None], (count, 128))
    starts = own_seg[0::tile]
    ends = own_seg[tile - 1 :: tile]
    low = jnp.sum((seg_row[None, :] < starts[:, None]).astype(jnp.int32), axis=1) // count
    high = (jnp.sum((seg_row[None, :] <= ends[:, None]).astype(jnp.int32), axis=1) - 1) // count + 1
    info = jnp.concatenate([me[None].astype(jnp.int32), low, high])
    seg_row = seg_row[None]

    near_qkv = far_rows(w_qkv, rep, size, reps, True)
    tokens_all = gather_near(tokens[0], size).reshape(seq_len, D)
    first_far = near_qkv[1][2]
    near_out = far_rows(w_out, rep, size, reps, False, first_far)
    near_up = far_rows(w_up, rep, size, reps, True, first_far)
    near_down = far_rows(w_down, rep, size, reps, True, near_up[1][2])
    qkv_full = gather_weight(w_qkv, near_qkv, me, size)
    out_full = gather_weight(w_out, near_out, me, size)
    up_full = gather_weight(w_up, near_up, me, size)
    down_full = gather_weight(w_down, near_down, me, size)

    normed_all = layer_norm(tokens_all.astype(F32), norm_gains[0], norm_shifts[0]).astype(BF16)
    shift = jnp.concatenate([proj_biases[0], jnp.zeros((D,), F32), proj_biases[1]])
    qkv_all = (add_rows(normed_all, qkv_full) + shift).astype(BF16)
    normed = normed_all[:count]
    source = tokens[0].astype(F32)

    attended_f, attended, lse, lse_row = attend(
        info, qkv_all, seg_col, seg_row, count, seq_len, size, tile
    )
    middle = source + add_rows(attended, out_full) + proj_biases[2]
    second = layer_norm(middle, norm_gains[1], norm_shifts[1]).astype(BF16)
    hidden_pre = add_rows(second, up_full) + up_bias
    hidden = jax.nn.gelu(hidden_pre).astype(BF16)

    upstream = cotangent[0]
    upstream_f = upstream.astype(F32)
    hidden_theirs, hidden_mine = by_core(hidden, me, size)
    down_theirs = other_grad([(hidden_theirs, upstream)])
    hidden_grad = back_rows(after(upstream, down_theirs), down_full)
    _, gelu_pull = jax.vjp(jax.nn.gelu, hidden_pre)
    pre_grad = gelu_pull(hidden_grad)[0].astype(BF16)
    down_part = core_grad(down_theirs, [(after(hidden_mine, pre_grad), upstream)], size)
    second_grad = back_rows(after(pre_grad, down_part), up_full)
    _, second_pull = jax.vjp(layer_norm, middle, norm_gains[1], norm_shifts[1])
    middle_part, gain_second, shift_second = second_pull(second_grad)
    middle_grad = upstream_f + middle_part
    branch_grad = middle_grad.astype(BF16)
    dout = back_rows(branch_grad, out_full).astype(BF16)
    row = lax.broadcasted_iota(jnp.int32, (8 * PAIRS, D), 0)
    minor = row % 8 - 2
    lane_head = lax.broadcasted_iota(jnp.int32, (8 * PAIRS, D), 1) // HD
    picks = ((row // 8 * 2 + minor == lane_head) & (minor >= 0) & (minor < 2)).astype(F32)
    delta_row = jnp.einsum(
        "ed,td->et", picks, dout.astype(F32) * attended_f, precision=lax.Precision.HIGHEST
    ).reshape(PAIRS, 8, count)
    stats = gather_later(lse_row + delta_row, size)
    dout_all = gather_later(dout, size).reshape(seq_len, D)

    second_theirs, second_mine = by_core(second, me, size)
    attended_theirs, attended_mine = by_core(attended, me, size)
    up_theirs = other_grad([(second_theirs, after(pre_grad, dout)), (attended_theirs, after(branch_grad, dout))])
    up_part = core_grad(up_theirs, [(second_mine, pre_grad), (attended_mine, branch_grad)], size)
    grad_down = spread_grad(down_part, me, rep, size, reps, (0,))
    grad_up_out = spread_grad(up_part, me, rep, size, reps, ())

    part = PAIRS // 2
    queries_one = query_grads(
        0, part, info, qkv_all, dout, attended_f, lse, seg_col, seg_row, count, seq_len, size, tile
    )
    queries_two = query_grads(
        part, part, info, qkv_all, after(dout, queries_one, up_part), attended_f, lse, seg_col, seg_row, count, seq_len, size, tile
    )
    keys_one, values_one = key_grads(
        0, part, info, qkv_all, after(dout_all, queries_two), stats, seg_col, seg_row, count, seq_len, size, tile
    )
    normed_theirs, normed_mine = by_core(normed, me, size)
    first_joined = jnp.concatenate([queries_one, queries_two, keys_one, values_one], axis=1)
    first_theirs = other_grad([(normed_theirs, first_joined)])
    keys_two, values_two = key_grads(
        part, part, info, qkv_all, after(dout_all, first_theirs), stats, seg_col, seg_row, count, seq_len, size, tile
    )
    first_part = core_grad(first_theirs, [(normed_mine, first_joined)], size)
    grad_first = spread_grad(first_part, me, rep, size, reps, ())
    last_joined = jnp.concatenate([keys_two, values_two], axis=1)
    last_theirs = other_grad([(normed_theirs, last_joined)])
    last_part = core_grad(last_theirs, [(normed_mine, last_joined)], size)

    joined_grad = jnp.concatenate(
        [queries_one, queries_two, keys_one, keys_two, values_one, values_two], axis=-1
    )
    normed_grad = back_rows(joined_grad, qkv_full)
    _, first_pull = jax.vjp(layer_norm, source, norm_gains[0], norm_shifts[0])
    source_part, gain_first, shift_first = first_pull(normed_grad)
    input_grad = middle_grad + source_part
    block_out = (middle + add_rows(hidden, down_full) + proj_biases[3]).astype(BF16)

    vectors = jnp.concatenate(
        [
            gain_first,
            gain_second,
            shift_first,
            shift_second,
            jnp.sum(joined_grad[:, :D].astype(F32), axis=0),
            jnp.sum(joined_grad[:, 2 * D :].astype(F32), axis=0),
            jnp.sum(branch_grad.astype(F32), axis=0),
            jnp.sum(upstream_f, axis=0),
            jnp.sum(pre_grad.astype(F32), axis=0),
        ]
    )
    grad_last, vectors = spread_last(last_part, vectors.reshape(-1, last_part.shape[2]), me, size, reps)
    vectors = vectors.reshape(-1)
    half = D // 2
    grad_qkv = jnp.concatenate(
        [grad_first[:, : D + half], grad_last[:, :half], grad_first[:, D + half :], grad_last[:, half:]], axis=1
    )
    grad_up, grad_out = grad_up_out[:, :FF], grad_up_out[:, FF:]
    return (
        block_out[None],
        input_grad[None],
        grad_qkv,
        grad_out,
        grad_up,
        grad_down,
        vectors[: 2 * D].reshape(2, D),
        vectors[2 * D : 4 * D].reshape(2, D),
        vectors[4 * D : 8 * D].reshape(4, D),
        vectors[8 * D :],
    )


def solution(mesh):
    return jax.shard_map(
        functools.partial(per_device, mesh.shape["rep"], mesh.shape["grp"]),
        mesh=mesh,
        in_specs=(
            P("rep", "grp", None),
            P("rep", None),
            P("grp", None),
            P("grp", None),
            P("grp", None),
            P("grp", None),
            P(),
            P(),
            P(),
            P(),
            P("rep", "grp", None),
        ),
        out_specs=(
            P("rep", "grp", None),
            P("rep", "grp", None),
            P("grp", None),
            P("grp", None),
            P("grp", None),
            P("grp", None),
            P(),
            P(),
            P(),
            P(),
        ),
        check_vma=False,
    )
```

profile of v0, /device:TPU:0, one launch (start us, length us, event | category | flops | bytes accessed | tf_op | source)
XLA Modules:
  0.0 484.0 jit_solution(754178041915944080)
XLA Ops:
  1.3 1.8 constant_dynamic-slice_fusion.12
  3.1 2.9 collective-permute-start.3
  8.3 2.0 constant_dynamic-slice_fusion.11
  11.0 2.0 broadcast_in_dim.35
  13.9 2.7 broadcast_in_dim.77
  20.6 2.0 collective-permute-start.8
  23.5 1.7 constant_dynamic-update-slice_fusion.23
  25.2 14.7 %collective-permute-done.8 = bf16[192,768]{1,0:T(8,128)(2,1)} collective-permute-done((bf16[192,768]{1,0:T(8,128)(2,1)S(1)}, bf16[192,768]{1,0:T(8,128)(2,1)}, u32[]{:S(2)}, u32[]{:S(2)}) %collective-permute-start.8) | collective-permute-done | bytes 294944 | tf_op jit(solution)/shard_map/ppermute | solution.py:42
  39.9 1.7 collective-permute-start.11
  41.7 1.7 constant_dynamic-update-slice_fusion.22
  45.1 2.3 constant_dynamic-update-slice_fusion.29
  47.4 1.8 constant_dynamic-update-slice_fusion.28
  49.2 5.4 %collective-permute-done.5 = bf16[96,2304]{1,0:T(8,128)(2,1)S(1)} collective-permute-done((bf16[96,2304]{1,0:T(8,128)(2,1)}, bf16[96,2304]{1,0:T(8,128)(2,1)S(1)}, u32[]{:S(2)}, u32[]{:S(2)}) %collective-permute-start.5) | collective-permute-done | bytes 442400 | tf_op jit(solution)/shard_map/ppermute | solution.py:42
  58.9 2.7 constant_dynamic-update-slice_fusion.19
  63.5 8.4 %collective-permute-done.16 = bf16[384,768]{1,0:T(8,128)(2,1)S(1)} collective-permute-done((bf16[384,768]{1,0:T(8,128)(2,1)S(1)}, bf16[384,768]{1,0:T(8,128)(2,1)S(1)}, u32[]{:S(2)}, u32[]{:S(2)}) %collective-permute-start.16) | collective-permute-done | bytes 589856 | tf_op jit(solution)/shard_map/ppermute | solution.py:42
  75.8 10.6 %collective-permute-done.18 = bf16[384,768]{1,0:T(8,128)(2,1)S(1)} collective-permute-done((bf16[384,768]{1,0:T(8,128)(2,1)S(1)}, bf16[384,768]{1,0:T(8,128)(2,1)S(1)}, u32[]{:S(2)}, u32[]{:S(2)}) %collective-permute-start.18) | collective-permute-done | bytes 589856 | tf_op jit(solution)/shard_map/ppermute | solution.py:42
  92.5 9.9 %add_convert_fusion.q_ref.k_ref.v_ref = bf16[2048,2304]{1,0:T(8,128)(2,1)S(1)} fusion(bf16[2048,768]{1,0:T(8,128)(2,1)S(1)} %fusion.10, bf16[768,2304]{1,0:T(8,128)(2,1)} %constant_dynamic-update-slice_fusion.25, f32[2304]{0:T(1024)S(1)} %pad_maximum_fusion.39), kind=kOutput, calls=%fused_computation | convolution fusion | flops 7257194496 | bytes 16131072 | tf_op jit(solution)/shard_map/dot_general | solution.py:30
  102.6 14.6 %shard_map.186 = (f32[512,768]{1,0:T(8,128)S(1)}, bf16[512,768]{1,0:T(8,128)(2,1)S(1)}, f32[512,768]{1,0:T(8,128)S(1)}, f32[6,8,512]{2,1,0:T(8,128)S(1)}) custom-call(s32[5]{0:T(128)S(1)} %pad_add_fusion.info, bf16[2048,2304]{1,0:T(8,128)(2,1)S(1)} %add_convert_fusion.q_ref.k_ref.v_ref, bf16[2048,2304]{1,0:T(8,128)(2,1)S(1)} %add_convert_fusion.q_ref.k_ref.v_ref, ...), custom_call_target="tpu_custom_call" | custom-call | flops 6442450944 | bytes 8388608 | tf_op jit(solution)/shard_map/pallas_call | solution.py:406
  118.8 8.7 %multiply_convert_fusion = (bf16[512,3072]{1,0:T(8,128)(2,1)S(1)}, f32[512,3072]{1,0:T(8,128)}) fusion(f32[3072]{0:T(1024)S(1)} %copy-done.67, bf16[512,768]{1,0:T(8,128)(2,1)S(1)} %add_convert_fusion.5, bf16[768,3072]{1,0:T(8,128)(2,1)} %constant_dynamic-update-slice_fusion.15), kind=kOutput, calls=%fused_computation.16 | convolution fusion | flops 2431647744 | bytes 14954496 | tf_op jit(solution)/shard_map/dot_general | solution.py:30
  128.6 2.9 convolution_convert_fusion.1
  132.5 5.4 %collective-permute-start.20 = (bf16[1536,768]{1,0:T(8,128)(2,1)}, bf16[1536,768]{1,0:T(8,128)(2,1)}, u32[]{:S(2)}, u32[]{:S(2)}) collective-permute-start(bf16[1536,768]{1,0:T(8,128)(2,1)} %convolution_convert_fusion.1), channel_id=1, source_target_pairs={{0,1},{1,0},{2,3},{3,2},{4,5},{5,4},{6,7},{7,6},{8,9},{9,8},{10,11... | collective-permute-start | bytes 7077896 | tf_op jit(solution)/shard_map/ppermute | solution.py:42
  139.7 2.1 copy-done.9
  141.9 9.7 %convert_reduce_fusion = (f32[3072]{0:T(1024)}, bf16[512,3072]{1,0:T(8,128)(2,1)S(1)}) fusion(f32[512,3072]{1,0:T(8,128)} %get-tuple-element.129, f32[3072]{0:T(1024)S(1)} %copy-done.67, bf16[512,768]{1,0:T(8,128)(2,1)S(1)} %bitcast.145, bf16[3072,768]{1,0:T(8,128)(2,1)} %copy-done.9), kind=kOutput, calls=%fused_computation.15 | convolution fusion | flops 2452091904 | bytes 14966784 | tf_op jit(solution)/shard_map/te,ce->tc/dot_general | solution.py:34
  151.6 3.7 fusion.43
  155.3 3.5 fusion.30
  158.8 3.1 add_convert_fusion.1
  161.9 6.8 %multiply_reduce_fusion.1 = (f32[768]{0:T(1024)}, f32[512]{0:T(512)S(1)}, f32[768]{0:T(1024)}, f32[512,768]{1,0:T(8,128)S(1)}) fusion(f32[512,768]{1,0:T(8,128)S(1)} %get-tuple-element.127, f32[512]{0:T(512)S(1)} %fusion.76, f32[512]{0:T(512)S(1)} %broadcast_multiply_fusion.2, f32[768]{0:T(1024)S(1)} %get-tuple-element.62, ...), kind=kOutput, calls=%fused_computation.57 | convolution fusion | flops 2419062784 | bytes 11025408 | tf_op jit(solution)/shard_map/te,ce->tc/dot_general | solution.py:34
  176.1 7.4 %shard_map.187 = bf16[512,384]{1,0:T(8,128)(2,1)S(1)} custom-call(s32[5]{0:T(128)S(1)} %pad_add_fusion.info, bf16[2048,2304]{1,0:T(8,128)(2,1)S(1)} %add_convert_fusion.q_ref.k_ref.v_ref, bf16[2048,2304]{1,0:T(8,128)(2,1)S(1)} %add_convert_fusion.q_ref.k_ref.v_ref, bf16[2048,2304]{1,0:T(8,128)(2,1)S(1)} %add_convert_fusion.q_ref.k_ref.v_ref, ...), custom_call_target="tpu_custom_call" | custom-call | flops 4831838208 | bytes 8388608 | tf_op jit(solution)/shard_map/pallas_call | solution.py:419
  186.5 1.7 fusion.41
  189.8 12.9 %collective-permute-done.44 = bf16[2,384,768]{2,1,0:T(8,128)(2,1)} collective-permute-done((bf16[2,384,768]{2,1,0:T(8,128)(2,1)S(1)}, bf16[2,384,768]{2,1,0:T(8,128)(2,1)}, u32[]{:S(2)}, u32[]{:S(2)}) %collective-permute-start.44) | collective-permute-done | bytes 1179680 | tf_op jit(solution)/shard_map/ppermute | solution.py:42
  204.2 5.5 %collective-permute-start.45 = (bf16[1,384,768]{2,1,0:T(8,128)(2,1)S(1)}, bf16[1,384,768]{2,1,0:T(8,128)(2,1)S(1)}, u32[]{:S(2)}, u32[]{:S(2)}) collective-permute-start(bf16[1,384,768]{2,1,0:T(8,128)(2,1)S(1)} %constant_dynamic-slice_fusion.2), channel_id=1, source_target_pairs={{0,2},{1,3},{2,0},{3,1},{4,6},{5,7},{6,4},{7,5},{8,10},{9,11},{10,... | collective-permute-start | bytes 1769480 | tf_op jit(solution)/shard_map/ppermute | solution.py:42
  209.7 1.8 pad_maximum_fusion.1
  211.8 11.8 %collective-permute-done.45 = bf16[1,384,768]{2,1,0:T(8,128)(2,1)S(1)} collective-permute-done((bf16[1,384,768]{2,1,0:T(8,128)(2,1)S(1)}, bf16[1,384,768]{2,1,0:T(8,128)(2,1)S(1)}, u32[]{:S(2)}, u32[]{:S(2)}) %collective-permute-start.45) | collective-permute-done | bytes 589856 | tf_op jit(solution)/shard_map/ppermute | solution.py:42
  223.8 21.1 %collective-permute-start.46 = (bf16[1,192,768]{2,1,0:T(8,128)(2,1)S(1)}, bf16[1,192,768]{2,1,0:T(8,128)(2,1)S(1)}, u32[]{:S(2)}, u32[]{:S(2)}) collective-permute-start(bf16[1,192,768]{2,1,0:T(8,128)(2,1)S(1)} %constant_dynamic-slice_fusion.1), channel_id=1, source_target_pairs={{0,8},{4,12},{8,0},{12,4},{16,24},{20,28},{24,16},{28,20},{1,9},{5... | collective-permute-start | bytes 884744 | tf_op jit(solution)/shard_map/ppermute | solution.py:42
  244.9 7.4 %shard_map.188 = bf16[512,384]{1,0:T(8,128)(2,1)S(1)} custom-call(s32[5]{0:T(128)S(1)} %pad_add_fusion.info, bf16[2048,2304]{1,0:T(8,128)(2,1)S(1)} %add_convert_fusion.q_ref.k_ref.v_ref, bf16[2048,2304]{1,0:T(8,128)(2,1)S(1)} %add_convert_fusion.q_ref.k_ref.v_ref, bf16[2048,2304]{1,0:T(8,128)(2,1)S(1)} %add_convert_fusion.q_ref.k_ref.v_ref, ...), custom_call_target="tpu_custom_call" | custom-call | flops 4831838208 | bytes 8388608 | tf_op jit(solution)/shard_map/pallas_call | solution.py:419
  252.2 2.3 collective-permute-start.36
  255.8 4.0 collective-permute-done.24
  259.9 5.8 %collective-permute-done.47 = bf16[1,96,768]{2,1,0:T(8,128)(2,1)S(1)} collective-permute-done((bf16[1,96,768]{2,1,0:T(8,128)(2,1)S(1)}, bf16[1,96,768]{2,1,0:T(8,128)(2,1)S(1)}, u32[]{:S(2)}, u32[]{:S(2)}) %collective-permute-start.47) | collective-permute-done | bytes 147488 | tf_op jit(solution)/shard_map/ppermute | solution.py:42
  266.2 9.4 %shard_map.189 = (bf16[512,384]{1,0:T(8,128)(2,1)S(1)}, bf16[512,384]{1,0:T(8,128)(2,1)S(1)}) custom-call(s32[5]{0:T(128)S(1)} %pad_add_fusion.info, bf16[2048,2304]{1,0:T(8,128)(2,1)S(1)} %add_convert_fusion.q_ref.k_ref.v_ref, bf16[2048,2304]{1,0:T(8,128)(2,1)S(1)} %add_convert_fusion.q_ref.k_ref.v_ref, ...), custom_call_target="tpu_custom_call" | custom-call | flops 6442450944 | bytes 8388608 | tf_op jit(solution)/shard_map/pallas_call | solution.py:435
  275.6 1.9 convolution_convert_fusion.2
  279.2 9.6 %shard_map.190 = (bf16[512,384]{1,0:T(8,128)(2,1)S(1)}, bf16[512,384]{1,0:T(8,128)(2,1)S(1)}) custom-call(s32[5]{0:T(128)S(1)} %pad_add_fusion.info, bf16[2048,2304]{1,0:T(8,128)(2,1)S(1)} %add_convert_fusion.q_ref.k_ref.v_ref, bf16[2048,2304]{1,0:T(8,128)(2,1)S(1)} %add_convert_fusion.q_ref.k_ref.v_ref, ...), custom_call_target="tpu_custom_call" | custom-call | flops 6442450944 | bytes 8388608 | tf_op jit(solution)/shard_map/pallas_call | solution.py:435
  289.5 4.3 fusion.97
  308.7 4.1 add_bitcast_fusion
  315.9 15.9 %collective-permute-start.50 = (bf16[1,384,768]{2,1,0:T(8,128)(2,1)}, bf16[1,384,768]{2,1,0:T(8,128)(2,1)}, u32[]{:S(2)}, u32[]{:S(2)}) collective-permute-start(bf16[1,384,768]{2,1,0:T(8,128)(2,1)} %pad_maximum_fusion.12), channel_id=1, source_target_pairs={{0,4},{4,0},{8,12},{12,8},{16,20},{20,16},{24,28},{28,24},{1,5},{5... | collective-permute-start | bytes 1769480 | tf_op jit(solution)/shard_map/ppermute | solution.py:42
  332.6 3.8 collective-permute-start.35
  336.4 2.6 fusion.11
  340.4 4.7 collective-permute-done.35
  345.2 2.2 add_convert_fusion.3
  349.3 2.1 collective-permute-start.26
  352.2 4.7 all-to-all-start
  359.9 28.7 %collective-permute-done.26 = bf16[1,192,1536]{2,1,0:T(8,128)(2,1)} collective-permute-done((bf16[1,192,1536]{2,1,0:T(8,128)(2,1)}, bf16[1,192,1536]{2,1,0:T(8,128)(2,1)}, u32[]{:S(2)}, u32[]{:S(2)}) %collective-permute-start.26) | collective-permute-done | bytes 589856 | tf_op jit(solution)/shard_map/ppermute | solution.py:42
  394.3 4.9 %collective-permute-done.27 = bf16[1,96,1536]{2,1,0:T(8,128)(2,1)} collective-permute-done((bf16[1,96,1536]{2,1,0:T(8,128)(2,1)}, bf16[1,96,1536]{2,1,0:T(8,128)(2,1)}, u32[]{:S(2)}, u32[]{:S(2)}) %collective-permute-start.27) | collective-permute-done | bytes 294944 | tf_op jit(solution)/shard_map/ppermute | solution.py:42
  400.4 5.3 %collective-permute-start.28 = (bf16[1,48,1536]{2,1,0:T(8,128)(2,1)S(1)}, bf16[1,48,1536]{2,1,0:T(8,128)(2,1)S(1)}, u32[]{:S(2)}, u32[]{:S(2)}) collective-permute-start(bf16[1,48,1536]{2,1,0:T(8,128)(2,1)S(1)} %constant_dynamic-slice_fusion.8), channel_id=1, source_target_pairs={{0,8},{4,12},{8,0},{12,4},{16,24},{20,28},{24,16},{28,20},{1,9},{5... | collective-permute-start | bytes 442376 | tf_op jit(solution)/shard_map/ppermute | solution.py:42
  405.7 1.8 fusion.12
  411.1 5.3 %all-to-all-start.1 = ((bf16[8,24,768]{2,1,0:T(8,128)(2,1)}), bf16[8,24,768]{2,1,0:T(8,128)(2,1)S(1)}, u32[]{:S(2)}, u32[]{:S(2)}) async-start(bf16[8,24,768]{2,1,0:T(8,128)(2,1)} %broadcast_in_dim.88), calls=%async_computation.1 | async-start | bytes 589824 | tf_op jit(solution)/shard_map/all_to_all | solution.py:191
  416.5 3.0 collective-permute-start.30
  419.4 9.5 %collective-permute-done.38 = bf16[1,96,3840]{2,1,0:T(8,128)(2,1)S(1)} collective-permute-done((bf16[1,96,3840]{2,1,0:T(8,128)(2,1)}, bf16[1,96,3840]{2,1,0:T(8,128)(2,1)S(1)}, u32[]{:S(2)}, u32[]{:S(2)}) %collective-permute-start.38) | collective-permute-done | bytes 737312 | tf_op jit(solution)/shard_map/ppermute | solution.py:42
  429.6 1.8 collective-permute-start.31
  431.4 8.6 %collective-permute-done.39 = bf16[1,48,3840]{2,1,0:T(8,128)(2,1)S(1)} collective-permute-done((bf16[1,48,3840]{2,1,0:T(8,128)(2,1)S(1)}, bf16[1,48,3840]{2,1,0:T(8,128)(2,1)S(1)}, u32[]{:S(2)}, u32[]{:S(2)}) %collective-permute-start.39) | collective-permute-done | bytes 368672 | tf_op jit(solution)/shard_map/ppermute | solution.py:42
  440.3 10.3 %collective-permute-done.40 = bf16[1,24,3840]{2,1,0:T(8,128)(2,1)S(1)} collective-permute-done((bf16[1,24,3840]{2,1,0:T(8,128)(2,1)S(1)}, bf16[1,24,3840]{2,1,0:T(8,128)(2,1)S(1)}, u32[]{:S(2)}, u32[]{:S(2)}) %collective-permute-start.40) | collective-permute-done | bytes 184352 | tf_op jit(solution)/shard_map/ppermute | solution.py:42
  450.8 7.1 %collective-permute-done.41 = bf16[1,24,3840]{2,1,0:T(8,128)(2,1)S(1)} collective-permute-done((bf16[1,24,3840]{2,1,0:T(8,128)(2,1)S(1)}, bf16[1,24,3840]{2,1,0:T(8,128)(2,1)S(1)}, u32[]{:S(2)}, u32[]{:S(2)}) %collective-permute-start.41) | collective-permute-done | bytes 184352 | tf_op jit(solution)/shard_map/ppermute | solution.py:42
  459.5 6.1 %collective-permute-done.42 = bf16[1,48,3840]{2,1,0:T(8,128)(2,1)S(1)} collective-permute-done((bf16[1,48,3840]{2,1,0:T(8,128)(2,1)S(1)}, bf16[1,48,3840]{2,1,0:T(8,128)(2,1)S(1)}, u32[]{:S(2)}, u32[]{:S(2)}) %collective-permute-start.42) | collective-permute-done | bytes 368672 | tf_op jit(solution)/shard_map/ppermute | solution.py:42
  469.7 11.1 %collective-permute-done.43 = bf16[1,96,3840]{2,1,0:T(8,128)(2,1)S(1)} collective-permute-done((bf16[1,96,3840]{2,1,0:T(8,128)(2,1)S(1)}, bf16[1,96,3840]{2,1,0:T(8,128)(2,1)S(1)}, u32[]{:S(2)}, u32[]{:S(2)}) %collective-permute-start.43) | collective-permute-done | bytes 737312 | tf_op jit(solution)/shard_map/ppermute | solution.py:42
  482.1 1.7 slice.213
  (370 shorter events, 94.3 us)
Async XLA Ops:
  0.7 22.6 %collective-permute-start.7 = (bf16[192,768]{1,0:T(8,128)(2,1)}, bf16[192,768]{1,0:T(8,128)(2,1)}, u32[]{:S(2)}, u32[]{:S(2)}) collective-permute-start(bf16[192,768]{1,0:T(8,128)(2,1)} %param.14), channel_id=1, source_target_pairs={{0,1},{1,0},{2,3},{3,2},{4,5},{5,4},{6,7},{7,6},{8,9},{9,8},{10,11... | collective-permute-start | bytes 884744 | tf_op jit(solution)/shard_map/ppermute | solution.py:42
  1.2 43.8 %collective-permute-start.2 = (bf16[192,2304]{1,0:T(8,128)(2,1)}, bf16[192,2304]{1,0:T(8,128)(2,1)}, u32[]{:S(2)}, u32[]{:S(2)}) collective-permute-start(bf16[192,2304]{1,0:T(8,128)(2,1)} %param.13), channel_id=1, source_target_pairs={{0,1},{1,0},{2,3},{3,2},{4,5},{5,4},{6,7},{7,6},{8,9},{9,8},{10,11... | collective-permute-start | bytes 2654216 | tf_op jit(solution)/shard_map/ppermute | solution.py:42
  3.1 17.5 %collective-permute-start.3 = (bf16[96,2304]{1,0:T(8,128)(2,1)}, bf16[96,2304]{1,0:T(8,128)(2,1)}, u32[]{:S(2)}, u32[]{:S(2)}) collective-permute-start(bf16[96,2304]{1,0:T(8,128)(2,1)} %constant_dynamic-slice_fusion.12), channel_id=1, source_target_pairs={{0,2},{1,3},{2,0},{3,1},{4,6},{5,7},{6,4},{7,5},{8,10},{9,11},{10,... | collective-permute-start | bytes 1327112 | tf_op jit(solution)/shard_map/ppermute | solution.py:42
  6.0 37.3 %collective-permute-start = (bf16[1,512,768]{2,1,0:T(8,128)(2,1)}, bf16[1,512,768]{2,1,0:T(8,128)(2,1)S(1)}, u32[]{:S(2)}, u32[]{:S(2)}) collective-permute-start(bf16[1,512,768]{2,1,0:T(8,128)(2,1)} %param.11), channel_id=1, source_target_pairs={{0,2},{1,3},{2,0},{3,1},{4,6},{5,7},{6,4},{7,5},{8,10},{9,11},{10,... | collective-permute-start | bytes 2359304 | tf_op jit(solution)/shard_map/ppermute | solution.py:42
  6.1 52.7 %collective-permute-start.10 = (bf16[192,3072]{1,0:T(8,128)(2,1)}, bf16[192,3072]{1,0:T(8,128)(2,1)}, u32[]{:S(2)}, u32[]{:S(2)}) collective-permute-start(bf16[192,3072]{1,0:T(8,128)(2,1)} %param.15), channel_id=1, source_target_pairs={{0,1},{1,0},{2,3},{3,2},{4,5},{5,4},{6,7},{7,6},{8,9},{9,8},{10,11... | collective-permute-start | bytes 3538952 | tf_op jit(solution)/shard_map/ppermute | solution.py:42
  20.6 19.4 %collective-permute-start.8 = (bf16[192,768]{1,0:T(8,128)(2,1)S(1)}, bf16[192,768]{1,0:T(8,128)(2,1)}, u32[]{:S(2)}, u32[]{:S(2)}) collective-permute-start(bf16[192,768]{1,0:T(8,128)(2,1)S(1)} %copy-done.39), channel_id=1, source_target_pairs={{0,2},{1,3},{2,0},{3,1},{4,6},{5,7},{6,4},{7,5},{8,10},{9,11},{10,... | collective-permute-start | bytes 884744 | tf_op jit(solution)/shard_map/ppermute | solution.py:42
  23.1 21.8 %copy-start.1 = (bf16[1,512,768]{2,1,0:T(8,128)(2,1)S(1)}, bf16[1,512,768]{2,1,0:T(8,128)(2,1)}, u32[]{:S(2)}) copy-start(bf16[1,512,768]{2,1,0:T(8,128)(2,1)} %param.11) | copy-start | bytes 2359300
  23.2 39.2 %collective-permute-start.15 = (bf16[768,768]{1,0:T(8,128)(2,1)S(1)}, bf16[768,768]{1,0:T(8,128)(2,1)S(1)}, u32[]{:S(2)}, u32[]{:S(2)}) collective-permute-start(bf16[768,768]{1,0:T(8,128)(2,1)S(1)} %copy-done.13), channel_id=1, source_target_pairs={{0,1},{1,0},{2,3},{3,2},{4,5},{5,4},{6,7},{7,6},{8,9},{9,8},{10,11... | collective-permute-start | bytes 3538952 | tf_op jit(solution)/shard_map/ppermute | solution.py:42
  39.9 16.8 %collective-permute-start.11 = (bf16[96,3072]{1,0:T(8,128)(2,1)S(1)}, bf16[96,3072]{1,0:T(8,128)(2,1)S(1)}, u32[]{:S(2)}, u32[]{:S(2)}) collective-permute-start(bf16[96,3072]{1,0:T(8,128)(2,1)S(1)} %copy-done.38), channel_id=1, source_target_pairs={{0,2},{1,3},{2,0},{3,1},{4,6},{5,7},{6,4},{7,5},{8,10},{9,11},{10,... | collective-permute-start | bytes 1769480 | tf_op jit(solution)/shard_map/ppermute | solution.py:42
  43.4 11.2 %collective-permute-start.5 = (bf16[96,2304]{1,0:T(8,128)(2,1)}, bf16[96,2304]{1,0:T(8,128)(2,1)S(1)}, u32[]{:S(2)}, u32[]{:S(2)}) collective-permute-start(bf16[96,2304]{1,0:T(8,128)(2,1)} %collective-permute-done.3), channel_id=1, source_target_pairs={{0,4},{4,0},{8,12},{12,8},{16,20},{20,16},{24,28},{28,24},{1,5},{5... | collective-permute-start | bytes 1327112 | tf_op jit(solution)/shard_map/ppermute | solution.py:42
  45.0 9.6 %collective-permute-start.4 = (bf16[96,2304]{1,0:T(8,128)(2,1)}, bf16[96,2304]{1,0:T(8,128)(2,1)S(1)}, u32[]{:S(2)}, u32[]{:S(2)}) collective-permute-start(bf16[96,2304]{1,0:T(8,128)(2,1)} %collective-permute-done.3), channel_id=1, source_target_pairs={{0,1},{1,0},{2,3},{3,2},{4,5},{5,4},{6,7},{7,6},{8,9},{9,8},{10,11... | collective-permute-start | bytes 1327112 | tf_op jit(solution)/shard_map/ppermute | solution.py:42
  54.6 2.7 collective-permute-start.9
  54.6 8.1 %collective-permute-start.6 = (bf16[96,2304]{1,0:T(8,128)(2,1)S(1)}, bf16[96,2304]{1,0:T(8,128)(2,1)S(1)}, u32[]{:S(2)}, u32[]{:S(2)}) collective-permute-start(bf16[96,2304]{1,0:T(8,128)(2,1)S(1)} %collective-permute-done.5), channel_id=1, source_target_pairs={{0,1},{1,0},{2,3},{3,2},{4,5},{5,4},{6,7},{7,6},{8,9},{9,8},{10,11... | collective-permute-start | bytes 1327112 | tf_op jit(solution)/shard_map/ppermute | solution.py:42
  56.7 15.2 %collective-permute-start.16 = (bf16[384,768]{1,0:T(8,128)(2,1)S(1)}, bf16[384,768]{1,0:T(8,128)(2,1)S(1)}, u32[]{:S(2)}, u32[]{:S(2)}) collective-permute-start(bf16[384,768]{1,0:T(8,128)(2,1)S(1)} %copy-done.37), channel_id=1, source_target_pairs={{0,2},{1,3},{2,0},{3,1},{4,6},{5,7},{6,4},{7,5},{8,10},{9,11},{10,... | collective-permute-start | bytes 1769480 | tf_op jit(solution)/shard_map/ppermute | solution.py:42
  57.3 16.1 %collective-permute-start.13 = (bf16[96,3072]{1,0:T(8,128)(2,1)S(1)}, bf16[96,3072]{1,0:T(8,128)(2,1)S(1)}, u32[]{:S(2)}, u32[]{:S(2)}) collective-permute-start(bf16[96,3072]{1,0:T(8,128)(2,1)S(1)} %collective-permute-done.11), channel_id=1, source_target_pairs={{0,4},{4,0},{8,12},{12,8},{16,20},{20,16},{24,28},{28,24},{1,5},{5... | collective-permute-start | bytes 1769480 | tf_op jit(solution)/shard_map/ppermute | solution.py:42
  58.8 58.5 %copy-start.29 = (bf16[768,768]{1,0:T(8,128)(2,1)}, bf16[768,768]{1,0:T(8,128)(2,1)S(1)}, u32[]{:S(2)}) copy-start(bf16[768,768]{1,0:T(8,128)(2,1)S(1)} %constant_dynamic-update-slice_fusion.21) | copy-start | bytes 3538948
  58.8 15.2 %collective-permute-start.12 = (bf16[96,3072]{1,0:T(8,128)(2,1)S(1)}, bf16[96,3072]{1,0:T(8,128)(2,1)S(1)}, u32[]{:S(2)}, u32[]{:S(2)}) collective-permute-start(bf16[96,3072]{1,0:T(8,128)(2,1)S(1)} %collective-permute-done.11), channel_id=1, source_target_pairs={{0,1},{1,0},{2,3},{3,2},{4,5},{5,4},{6,7},{7,6},{8,9},{9,8},{10,11... | collective-permute-start | bytes 1769480 | tf_op jit(solution)/shard_map/ppermute | solution.py:42
  62.5 24.9 %collective-permute-start.1 = (bf16[2,512,768]{2,1,0:T(8,128)(2,1)S(1)}, bf16[2,512,768]{2,1,0:T(8,128)(2,1)S(1)}, u32[]{:S(2)}, u32[]{:S(2)}) collective-permute-start(bf16[2,512,768]{2,1,0:T(8,128)(2,1)S(1)} %pad_maximum_fusion.3), channel_id=1, source_target_pairs={{0,1},{1,0},{2,3},{3,2},{4,5},{5,4},{6,7},{7,6},{8,9},{9,8},{10,11... | collective-permute-start | bytes 4718600 | tf_op jit(solution)/shard_map/ppermute | solution.py:42
  72.0 14.4 %collective-permute-start.18 = (bf16[384,768]{1,0:T(8,128)(2,1)S(1)}, bf16[384,768]{1,0:T(8,128)(2,1)S(1)}, u32[]{:S(2)}, u32[]{:S(2)}) collective-permute-start(bf16[384,768]{1,0:T(8,128)(2,1)S(1)} %collective-permute-done.16), channel_id=1, source_target_pairs={{0,4},{4,0},{8,12},{12,8},{16,20},{20,16},{24,28},{28,24},{1,5},{5... | collective-permute-start | bytes 1769480 | tf_op jit(solution)/shard_map/ppermute | solution.py:42
  73.5 12.9 %collective-permute-start.17 = (bf16[384,768]{1,0:T(8,128)(2,1)S(1)}, bf16[384,768]{1,0:T(8,128)(2,1)S(1)}, u32[]{:S(2)}, u32[]{:S(2)}) collective-permute-start(bf16[384,768]{1,0:T(8,128)(2,1)S(1)} %collective-permute-done.16), channel_id=1, source_target_pairs={{0,1},{1,0},{2,3},{3,2},{4,5},{5,4},{6,7},{7,6},{8,9},{9,8},{10,11... | collective-permute-start | bytes 1769480 | tf_op jit(solution)/shard_map/ppermute | solution.py:42
  73.5 13.0 %collective-permute-start.14 = (bf16[96,3072]{1,0:T(8,128)(2,1)S(1)}, bf16[96,3072]{1,0:T(8,128)(2,1)S(1)}, u32[]{:S(2)}, u32[]{:S(2)}) collective-permute-start(bf16[96,3072]{1,0:T(8,128)(2,1)S(1)} %collective-permute-done.13), channel_id=1, source_target_pairs={{0,1},{1,0},{2,3},{3,2},{4,5},{5,4},{6,7},{7,6},{8,9},{9,8},{10,11... | collective-permute-start | bytes 1769480 | tf_op jit(solution)/shard_map/ppermute | solution.py:42
  86.4 53.3 %collective-permute-start.19 = (bf16[384,768]{1,0:T(8,128)(2,1)S(1)}, bf16[384,768]{1,0:T(8,128)(2,1)S(1)}, u32[]{:S(2)}, u32[]{:S(2)}) collective-permute-start(bf16[384,768]{1,0:T(8,128)(2,1)S(1)} %collective-permute-done.18), channel_id=1, source_target_pairs={{0,1},{1,0},{2,3},{3,2},{4,5},{5,4},{6,7},{7,6},{8,9},{9,8},{10,11... | collective-permute-start | bytes 1769480 | tf_op jit(solution)/shard_map/ppermute | solution.py:42
  132.5 53.3 %copy-start.33 = (bf16[512,192]{1,0:T(8,128)(2,1)}, bf16[512,192]{1,0:T(8,128)(2,1)S(1)}, u32[]{:S(2)}) copy-start(bf16[512,192]{1,0:T(8,128)(2,1)S(1)} %get-tuple-element.93) | copy-start | bytes 589828
  132.5 53.3 %copy-start.34 = (bf16[512,192]{1,0:T(8,128)(2,1)}, bf16[512,192]{1,0:T(8,128)(2,1)S(1)}, u32[]{:S(2)}) copy-start(bf16[512,192]{1,0:T(8,128)(2,1)S(1)} %get-tuple-element.94) | copy-start | bytes 589828
  132.5 26.3 %collective-permute-start.20 = (bf16[1536,768]{1,0:T(8,128)(2,1)}, bf16[1536,768]{1,0:T(8,128)(2,1)}, u32[]{:S(2)}, u32[]{:S(2)}) collective-permute-start(bf16[1536,768]{1,0:T(8,128)(2,1)} %convolution_convert_fusion.1), channel_id=1, source_target_pairs={{0,1},{1,0},{2,3},{3,2},{4,5},{5,4},{6,7},{7,6},{8,9},{9,8},{10,11... | collective-permute-start | bytes 7077896 | tf_op jit(solution)/shard_map/ppermute | solution.py:42
  173.2 82.2 %collective-permute-start.23 = (f32[1,6,8,512]{3,2,1,0:T(8,128)S(1)}, f32[1,6,8,512]{3,2,1,0:T(8,128)S(1)}, u32[]{:S(2)}, u32[]{:S(2)}) collective-permute-start(f32[1,6,8,512]{3,2,1,0:T(8,128)S(1)} %add_bitcast_fusion.1), channel_id=1, source_target_pairs={{2,0},{3,1},{6,4},{7,5},{10,8},{11,9},{14,12},{15,13},{18,16},{19,... | collective-permute-start | bytes 294920 | tf_op jit(solution)/shard_map/ppermute | solution.py:64
  174.6 28.0 %collective-permute-start.44 = (bf16[2,384,768]{2,1,0:T(8,128)(2,1)S(1)}, bf16[2,384,768]{2,1,0:T(8,128)(2,1)}, u32[]{:S(2)}, u32[]{:S(2)}) collective-permute-start(bf16[2,384,768]{2,1,0:T(8,128)(2,1)S(1)} %constant_dynamic-slice_fusion.3), channel_id=1, source_target_pairs={{0,4},{4,0},{8,12},{12,8},{16,20},{20,16},{24,28},{28,24},{1,5},{5... | collective-permute-start | bytes 3538952 | tf_op jit(solution)/shard_map/ppermute | solution.py:42
  183.5 28.0 %collective-permute-start.21 = (bf16[1,512,768]{2,1,0:T(8,128)(2,1)S(1)}, bf16[1,512,768]{2,1,0:T(8,128)(2,1)S(1)}, u32[]{:S(2)}, u32[]{:S(2)}) collective-permute-start(bf16[1,512,768]{2,1,0:T(8,128)(2,1)S(1)} %bitcast.137), channel_id=1, source_target_pairs={{2,0},{3,1},{6,4},{7,5},{10,8},{11,9},{14,12},{15,13},{18,16},{19,... | collective-permute-start | bytes 2359304 | tf_op jit(solution)/shard_map/ppermute | solution.py:64
  204.2 19.3 %collective-permute-start.45 = (bf16[1,384,768]{2,1,0:T(8,128)(2,1)S(1)}, bf16[1,384,768]{2,1,0:T(8,128)(2,1)S(1)}, u32[]{:S(2)}, u32[]{:S(2)}) collective-permute-start(bf16[1,384,768]{2,1,0:T(8,128)(2,1)S(1)} %constant_dynamic-slice_fusion.2), channel_id=1, source_target_pairs={{0,2},{1,3},{2,0},{3,1},{4,6},{5,7},{6,4},{7,5},{8,10},{9,11},{10,... | collective-permute-start | bytes 1769480 | tf_op jit(solution)/shard_map/ppermute | solution.py:42
  211.7 54.1 %collective-permute-start.22 = (bf16[2,512,768]{2,1,0:T(8,128)(2,1)S(1)}, bf16[2,512,768]{2,1,0:T(8,128)(2,1)S(1)}, u32[]{:S(2)}, u32[]{:S(2)}) collective-permute-start(bf16[2,512,768]{2,1,0:T(8,128)(2,1)S(1)} %pad_maximum_fusion.6), channel_id=1, source_target_pairs={{0,1},{1,0},{2,3},{3,2},{4,5},{5,4},{6,7},{7,6},{8,9},{9,8},{10,11... | collective-permute-start | bytes 4718600 | tf_op jit(solution)/shard_map/ppermute | solution.py:64
  223.8 31.7 %collective-permute-start.46 = (bf16[1,192,768]{2,1,0:T(8,128)(2,1)S(1)}, bf16[1,192,768]{2,1,0:T(8,128)(2,1)S(1)}, u32[]{:S(2)}, u32[]{:S(2)}) collective-permute-start(bf16[1,192,768]{2,1,0:T(8,128)(2,1)S(1)} %constant_dynamic-slice_fusion.1), channel_id=1, source_target_pairs={{0,8},{4,12},{8,0},{12,4},{16,24},{20,28},{24,16},{28,20},{1,9},{5... | collective-permute-start | bytes 884744 | tf_op jit(solution)/shard_map/ppermute | solution.py:42
  252.2 84.2 %collective-permute-start.36 = (bf16[384,3840]{1,0:T(8,128)(2,1)}, bf16[384,3840]{1,0:T(8,128)(2,1)}, u32[]{:S(2)}, u32[]{:S(2)}) collective-permute-start(bf16[384,3840]{1,0:T(8,128)(2,1)} %pad_maximum_fusion.1), channel_id=1, source_target_pairs={{0,1},{1,0},{2,3},{3,2},{4,5},{5,4},{6,7},{7,6},{8,9},{9,8},{10,11... | collective-permute-start | bytes 8847368 | tf_op jit(solution)/shard_map/ppermute | solution.py:42
  255.4 4.5 collective-permute-start.24
  255.6 10.1 %collective-permute-start.47 = (bf16[1,96,768]{2,1,0:T(8,128)(2,1)S(1)}, bf16[1,96,768]{2,1,0:T(8,128)(2,1)S(1)}, u32[]{:S(2)}, u32[]{:S(2)}) collective-permute-start(bf16[1,96,768]{2,1,0:T(8,128)(2,1)S(1)} %constant_dynamic-slice_fusion), channel_id=1, source_target_pairs={{0,16},{4,20},{8,24},{12,28},{16,0},{20,4},{24,8},{28,12},{1,17},{... | collective-permute-start | bytes 442376 | tf_op jit(solution)/shard_map/ppermute | solution.py:42
  265.7 11.8 %collective-permute-start.48 = (bf16[1,96,768]{2,1,0:T(8,128)(2,1)S(1)}, bf16[1,96,768]{2,1,0:T(8,128)(2,1)S(1)}, u32[]{:S(2)}, u32[]{:S(2)}) collective-permute-start(bf16[1,96,768]{2,1,0:T(8,128)(2,1)S(1)} %add_convert_fusion.13), channel_id=1, source_target_pairs={{0,16},{4,20},{8,24},{12,28},{16,0},{20,4},{24,8},{28,12},{1,17},{... | collective-permute-start | bytes 442376 | tf_op jit(solution)/shard_map/ppermute | solution.py:42
  277.5 67.6 %collective-permute-start.25 = (bf16[384,1536]{1,0:T(8,128)(2,1)}, bf16[384,1536]{1,0:T(8,128)(2,1)}, u32[]{:S(2)}, u32[]{:S(2)}) collective-permute-start(bf16[384,1536]{1,0:T(8,128)(2,1)} %convolution_convert_fusion.2), channel_id=1, source_target_pairs={{0,1},{1,0},{2,3},{3,2},{4,5},{5,4},{6,7},{7,6},{8,9},{9,8},{10,11... | collective-permute-start | bytes 3538952 | tf_op jit(solution)/shard_map/ppermute | solution.py:42
  278.4 35.5 %collective-permute-start.49 = (bf16[1,192,768]{2,1,0:T(8,128)(2,1)}, bf16[1,192,768]{2,1,0:T(8,128)(2,1)}, u32[]{:S(2)}, u32[]{:S(2)}) collective-permute-start(bf16[1,192,768]{2,1,0:T(8,128)(2,1)} %pad_maximum_fusion.23), channel_id=1, source_target_pairs={{0,8},{4,12},{8,0},{12,4},{16,24},{20,28},{24,16},{28,20},{1,9},{5... | collective-permute-start | bytes 884744 | tf_op jit(solution)/shard_map/ppermute | solution.py:42
  307.7 6.2 %collective-permute-start.34 = (f32[12,768]{1,0:T(8,128)}, f32[12,768]{1,0:T(8,128)S(1)}, u32[]{:S(2)}, u32[]{:S(2)}) collective-permute-start(f32[12,768]{1,0:T(8,128)} %reshape.210), channel_id=1, source_target_pairs={{0,1},{1,0},{2,3},{3,2},{4,5},{5,4},{6,7},{7,6},{8,9},{9,8},{10,11... | collective-permute-start | bytes 110600 | tf_op jit(solution)/shard_map/ppermute | solution.py:42
  308.7 27.7 %slice-start = ((s8[4718592]{0:T(1024)(128)(4,1)}), s8[4194304]{0:T(1024)(128)(4,1)S(1)}, s32[]{:S(2)}) async-start(s8[4718592]{0:T(1024)(128)(4,1)} %bitcast.141), calls=%async_computation.2 | async-start | bytes 8388608
  312.9 23.6 %slice-start.1 = ((s8[4718592]{0:T(1024)(128)(4,1)}), s8[524288]{0:T(1024)(128)(4,1)S(1)}, s32[]{:S(2)}) async-start(s8[4718592]{0:T(1024)(128)(4,1)} %bitcast.141), calls=%async_computation.3 | async-start | bytes 1048576
  313.5 18.3 %collective-permute-start.33 = (bf16[384,768]{1,0:T(8,128)(2,1)S(1)}, bf16[384,768]{1,0:T(8,128)(2,1)S(1)}, u32[]{:S(2)}, u32[]{:S(2)}) collective-permute-start(bf16[384,768]{1,0:T(8,128)(2,1)S(1)} %convolution_convert_fusion.5), channel_id=1, source_target_pairs={{0,1},{1,0},{2,3},{3,2},{4,5},{5,4},{6,7},{7,6},{8,9},{9,8},{10,11... | collective-permute-start | bytes 1769480 | tf_op jit(solution)/shard_map/ppermute | solution.py:42
  315.0 17.5 %copy-start.14 = (bf16[1,192,768]{2,1,0:T(8,128)(2,1)}, bf16[1,192,768]{2,1,0:T(8,128)(2,1)S(1)}, u32[]{:S(2)}) copy-start(bf16[1,192,768]{2,1,0:T(8,128)(2,1)S(1)} %get-tuple-element.100) | copy-start | bytes 884740
  315.0 17.5 %copy-start.16 = (bf16[1,192,768]{2,1,0:T(8,128)(2,1)}, bf16[1,192,768]{2,1,0:T(8,128)(2,1)S(1)}, u32[]{:S(2)}) copy-start(bf16[1,192,768]{2,1,0:T(8,128)(2,1)S(1)} %get-tuple-element.101) | copy-start | bytes 884740
  315.9 41.0 %collective-permute-start.50 = (bf16[1,384,768]{2,1,0:T(8,128)(2,1)}, bf16[1,384,768]{2,1,0:T(8,128)(2,1)}, u32[]{:S(2)}, u32[]{:S(2)}) collective-permute-start(bf16[1,384,768]{2,1,0:T(8,128)(2,1)} %pad_maximum_fusion.12), channel_id=1, source_target_pairs={{0,4},{4,0},{8,12},{12,8},{16,20},{20,16},{24,28},{28,24},{1,5},{5... | collective-permute-start | bytes 1769480 | tf_op jit(solution)/shard_map/ppermute | solution.py:42
  332.6 12.5 %collective-permute-start.35 = (bf16[216,768]{1,0:T(8,128)(2,1)S(1)}, bf16[216,768]{1,0:T(8,128)(2,1)S(1)}, u32[]{:S(2)}, u32[]{:S(2)}) collective-permute-start(bf16[216,768]{1,0:T(8,128)(2,1)S(1)} %pad_maximum_fusion.21), channel_id=1, source_target_pairs={{0,2},{1,3},{2,0},{3,1},{4,6},{5,7},{6,4},{7,5},{8,10},{9,11},{10,... | collective-permute-start | bytes 995336 | tf_op jit(solution)/shard_map/ppermute | solution.py:42
  340.4 65.4 %collective-permute-start.37 = (bf16[1,192,3840]{2,1,0:T(8,128)(2,1)}, bf16[1,192,3840]{2,1,0:T(8,128)(2,1)}, u32[]{:S(2)}, u32[]{:S(2)}) collective-permute-start(bf16[1,192,3840]{2,1,0:T(8,128)(2,1)} %dynamic-slice_bitcast_fusion), channel_id=1, source_target_pairs={{0,2},{1,3},{2,0},{3,1},{4,6},{5,7},{6,4},{7,5},{8,10},{9,11},{10,... | collective-permute-start | bytes 4423688 | tf_op jit(solution)/shard_map/ppermute | solution.py:42
  349.3 39.3 %collective-permute-start.26 = (bf16[1,192,1536]{2,1,0:T(8,128)(2,1)}, bf16[1,192,1536]{2,1,0:T(8,128)(2,1)}, u32[]{:S(2)}, u32[]{:S(2)}) collective-permute-start(bf16[1,192,1536]{2,1,0:T(8,128)(2,1)} %dynamic-slice_bitcast_fusion.1), channel_id=1, source_target_pairs={{0,2},{1,3},{2,0},{3,1},{4,6},{5,7},{6,4},{7,5},{8,10},{9,11},{10,... | collective-permute-start | bytes 1769480 | tf_op jit(solution)/shard_map/ppermute | solution.py:42
  352.2 38.8 %all-to-all-start = ((bf16[8,48,768]{2,1,0:T(8,128)(2,1)}), bf16[8,48,768]{2,1,0:T(8,128)(2,1)S(1)}, u32[]{:S(2)}, u32[]{:S(2)}) async-start(bf16[8,48,768]{2,1,0:T(8,128)(2,1)} %pad_maximum_fusion.11), calls=%async_computation | async-start | bytes 1179648 | tf_op jit(solution)/shard_map/all_to_all | solution.py:188
  358.3 30.3 %copy-start.32 = (bf16[384,1536]{1,0:T(8,128)(2,1)S(1)}, bf16[384,1536]{1,0:T(8,128)(2,1)}, u32[]{:S(2)}) copy-start(bf16[384,1536]{1,0:T(8,128)(2,1)} %copy-done.31) | copy-start | bytes 3538948
  359.8 45.9 %copy-start.5 = (bf16[384,3840]{1,0:T(8,128)(2,1)S(1)}, bf16[384,3840]{1,0:T(8,128)(2,1)}, u32[]{:S(2)}) copy-start(bf16[384,3840]{1,0:T(8,128)(2,1)} %copy-done.4) | copy-start | bytes 8847364
  390.7 8.5 %collective-permute-start.27 = (bf16[1,96,1536]{2,1,0:T(8,128)(2,1)}, bf16[1,96,1536]{2,1,0:T(8,128)(2,1)}, u32[]{:S(2)}, u32[]{:S(2)}) collective-permute-start(bf16[1,96,1536]{2,1,0:T(8,128)(2,1)} %constant_dynamic-slice_fusion.9), channel_id=1, source_target_pairs={{0,4},{4,0},{8,12},{12,8},{16,20},{20,16},{24,28},{28,24},{1,5},{5... | collective-permute-start | bytes 884744 | tf_op jit(solution)/shard_map/ppermute | solution.py:42
  400.4 9.7 %collective-permute-start.28 = (bf16[1,48,1536]{2,1,0:T(8,128)(2,1)S(1)}, bf16[1,48,1536]{2,1,0:T(8,128)(2,1)S(1)}, u32[]{:S(2)}, u32[]{:S(2)}) collective-permute-start(bf16[1,48,1536]{2,1,0:T(8,128)(2,1)S(1)} %constant_dynamic-slice_fusion.8), channel_id=1, source_target_pairs={{0,8},{4,12},{8,0},{12,4},{16,24},{20,28},{24,16},{28,20},{1,9},{5... | collective-permute-start | bytes 442376 | tf_op jit(solution)/shard_map/ppermute | solution.py:42
  409.5 19.4 %copy-start.8 = (bf16[1,192,3840]{2,1,0:T(8,128)(2,1)S(1)}, bf16[1,192,3840]{2,1,0:T(8,128)(2,1)}, u32[]{:S(2)}) copy-start(bf16[1,192,3840]{2,1,0:T(8,128)(2,1)} %copy-done.7) | copy-start | bytes 4423684
  409.5 19.4 %collective-permute-start.38 = (bf16[1,96,3840]{2,1,0:T(8,128)(2,1)}, bf16[1,96,3840]{2,1,0:T(8,128)(2,1)S(1)}, u32[]{:S(2)}, u32[]{:S(2)}) collective-permute-start(bf16[1,96,3840]{2,1,0:T(8,128)(2,1)} %constant_dynamic-slice_fusion.6), channel_id=1, source_target_pairs={{0,4},{4,0},{8,12},{12,8},{16,20},{20,16},{24,28},{28,24},{1,5},{5... | collective-permute-start | bytes 2211848 | tf_op jit(solution)/shard_map/ppermute | solution.py:42
  410.2 6.2 %collective-permute-start.29 = (bf16[1,24,1536]{2,1,0:T(8,128)(2,1)S(1)}, bf16[1,24,1536]{2,1,0:T(8,128)(2,1)S(1)}, u32[]{:S(2)}, u32[]{:S(2)}) collective-permute-start(bf16[1,24,1536]{2,1,0:T(8,128)(2,1)S(1)} %constant_dynamic-slice_fusion.7), channel_id=1, source_target_pairs={{0,16},{4,20},{8,24},{12,28},{16,0},{20,4},{24,8},{28,12},{1,17},{... | collective-permute-start | bytes 221192 | tf_op jit(solution)/shard_map/ppermute | solution.py:42
  411.1 29.1 %all-to-all-start.1 = ((bf16[8,24,768]{2,1,0:T(8,128)(2,1)}), bf16[8,24,768]{2,1,0:T(8,128)(2,1)S(1)}, u32[]{:S(2)}, u32[]{:S(2)}) async-start(bf16[8,24,768]{2,1,0:T(8,128)(2,1)} %broadcast_in_dim.88), calls=%async_computation.1 | async-start | bytes 589824 | tf_op jit(solution)/shard_map/all_to_all | solution.py:191
  416.5 13.1 %collective-permute-start.30 = (bf16[1,24,1536]{2,1,0:T(8,128)(2,1)S(1)}, bf16[1,24,1536]{2,1,0:T(8,128)(2,1)S(1)}, u32[]{:S(2)}, u32[]{:S(2)}) collective-permute-start(bf16[1,24,1536]{2,1,0:T(8,128)(2,1)S(1)} %add_convert_fusion.15), channel_id=1, source_target_pairs={{0,16},{4,20},{8,24},{12,28},{16,0},{20,4},{24,8},{28,12},{1,17},{... | collective-permute-start | bytes 221192 | tf_op jit(solution)/shard_map/ppermute | solution.py:42
  429.2 10.8 %collective-permute-start.39 = (bf16[1,48,3840]{2,1,0:T(8,128)(2,1)S(1)}, bf16[1,48,3840]{2,1,0:T(8,128)(2,1)S(1)}, u32[]{:S(2)}, u32[]{:S(2)}) collective-permute-start(bf16[1,48,3840]{2,1,0:T(8,128)(2,1)S(1)} %constant_dynamic-slice_fusion.5), channel_id=1, source_target_pairs={{0,8},{4,12},{8,0},{12,4},{16,24},{20,28},{24,16},{28,20},{1,9},{5... | collective-permute-start | bytes 1105928 | tf_op jit(solution)/shard_map/ppermute | solution.py:42
  429.6 28.5 %collective-permute-start.31 = (bf16[1,48,1536]{2,1,0:T(8,128)(2,1)S(1)}, bf16[1,48,1536]{2,1,0:T(8,128)(2,1)S(1)}, u32[]{:S(2)}, u32[]{:S(2)}) collective-permute-start(bf16[1,48,1536]{2,1,0:T(8,128)(2,1)S(1)} %pad_maximum_fusion.37), channel_id=1, source_target_pairs={{0,8},{4,12},{8,0},{12,4},{16,24},{20,28},{24,16},{28,20},{1,9},{5... | collective-permute-start | bytes 442376 | tf_op jit(solution)/shard_map/ppermute | solution.py:42
  440.1 10.5 %collective-permute-start.40 = (bf16[1,24,3840]{2,1,0:T(8,128)(2,1)S(1)}, bf16[1,24,3840]{2,1,0:T(8,128)(2,1)S(1)}, u32[]{:S(2)}, u32[]{:S(2)}) collective-permute-start(bf16[1,24,3840]{2,1,0:T(8,128)(2,1)S(1)} %constant_dynamic-slice_fusion.4), channel_id=1, source_target_pairs={{0,16},{4,20},{8,24},{12,28},{16,0},{20,4},{24,8},{28,12},{1,17},{... | collective-permute-start | bytes 552968 | tf_op jit(solution)/shard_map/ppermute | solution.py:42
  450.7 7.3 %collective-permute-start.41 = (bf16[1,24,3840]{2,1,0:T(8,128)(2,1)S(1)}, bf16[1,24,3840]{2,1,0:T(8,128)(2,1)S(1)}, u32[]{:S(2)}, u32[]{:S(2)}) collective-permute-start(bf16[1,24,3840]{2,1,0:T(8,128)(2,1)S(1)} %add_convert_fusion.12), channel_id=1, source_target_pairs={{0,16},{4,20},{8,24},{12,28},{16,0},{20,4},{24,8},{28,12},{1,17},{... | collective-permute-start | bytes 552968 | tf_op jit(solution)/shard_map/ppermute | solution.py:42
  458.0 7.6 %collective-permute-start.42 = (bf16[1,48,3840]{2,1,0:T(8,128)(2,1)S(1)}, bf16[1,48,3840]{2,1,0:T(8,128)(2,1)S(1)}, u32[]{:S(2)}, u32[]{:S(2)}) collective-permute-start(bf16[1,48,3840]{2,1,0:T(8,128)(2,1)S(1)} %pad_maximum_fusion.20), channel_id=1, source_target_pairs={{0,8},{4,12},{8,0},{12,4},{16,24},{20,28},{24,16},{28,20},{1,9},{5... | collective-permute-start | bytes 1105928 | tf_op jit(solution)/shard_map/ppermute | solution.py:42
  458.2 9.8 %collective-permute-start.32 = (bf16[1,96,1536]{2,1,0:T(8,128)(2,1)S(1)}, bf16[1,96,1536]{2,1,0:T(8,128)(2,1)S(1)}, u32[]{:S(2)}, u32[]{:S(2)}) collective-permute-start(bf16[1,96,1536]{2,1,0:T(8,128)(2,1)S(1)} %pad_maximum_fusion.22), channel_id=1, source_target_pairs={{0,4},{4,0},{8,12},{12,8},{16,20},{20,16},{24,28},{28,24},{1,5},{5... | collective-permute-start | bytes 884744 | tf_op jit(solution)/shard_map/ppermute | solution.py:42
  465.8 15.0 %collective-permute-start.43 = (bf16[1,96,3840]{2,1,0:T(8,128)(2,1)S(1)}, bf16[1,96,3840]{2,1,0:T(8,128)(2,1)S(1)}, u32[]{:S(2)}, u32[]{:S(2)}) collective-permute-start(bf16[1,96,3840]{2,1,0:T(8,128)(2,1)S(1)} %pad_maximum_fusion.10), channel_id=1, source_target_pairs={{0,4},{4,0},{8,12},{12,8},{16,20},{20,16},{24,28},{28,24},{1,5},{5... | collective-permute-start | bytes 2211848 | tf_op jit(solution)/shard_map/ppermute | solution.py:42
  (59 other events, 329.8 us)
where the time goes:
time: 487 us; the launch traced here: 484 us
  waiting for transfers between devices  166 us (34%)
  starting transfers between devices  100 us (21%)
  matrix products  64.6 us (13%)
  local copies, waits for them, and re-layouts  64.2 us (13%)
  Pallas kernels  48.3 us (10%)
  other arithmetic  38.3 us (8%)
    ppermute x47, waiting for transfers between devices, swap(): return lax.ppermute(value, axis, [(i, i ^ mask) for i in range(size)])  162 us
    ppermute x47, starting transfers between devices, swap(): return lax.ppermute(value, axis, [(i, i ^ mask) for i in range(size)])  87.3 us
    dot_general x4, matrix products, add_rows(): return jnp.dot(left, piece, preferred_element_type=F32)  23 us
    dot_general x4, matrix products, back_rows(): return jnp.einsum('te,ce->tc', right, piece, preferred_element_type=F32)  21.5 us
    unnamed x155, local copies, waits for them, and re-layouts  19.7 us
    dot_general x10, matrix products, token_product(): return jnp.einsum('tc,te->ce', left, right, preferred_element_type=F32)  19.1 us
    pallas_call x2, Pallas kernels, key_grads(): call(functools.partial(key_grad_kernel, size, tile), [strip(count, PAIRS...  18.9 us
    pallas_call x2, Pallas kernels, query_grads(): call(functools.partial(query_grad_kernel, size, tile), [strip(count, firs...  14.8 us
  transfers between devices with their start and end apart: 53, of which 18 were waited for; matrix products, arithmetic and copies ran while one was open for 30% of the time, Pallas kernels for 10%

commit v1 on v0

v1 whole, which is shorter than its diff:
```python
import functools
import math

import jax
import jax.numpy as jnp
from jax import lax
from jax.experimental import pallas as pl
from jax.experimental.pallas import tpu as pltpu
from jax.sharding import PartitionSpec as P

D = 768
H = 12
HD = 64
FF = 3072
PAIRS = H // 2
LANES = 2 * HD
NEG = -1e30
SCALE = 1.0 / math.sqrt(HD)
F32 = jnp.float32
BF16 = jnp.bfloat16


def layer_norm(values, gain_row, shift_row):
    centre = values - jnp.mean(values, axis=-1, keepdims=True)
    spread = jnp.mean(centre * centre, axis=-1, keepdims=True)
    return centre * lax.rsqrt(spread + 1e-05) * gain_row + shift_row


def add_rows(left, piece):
    return jnp.dot(left, piece, preferred_element_type=F32)


def back_rows(right, piece):
    return jnp.einsum("te,ce->tc", right, piece, preferred_element_type=F32)


def token_product(left, right):
    return jnp.einsum("tc,te->ce", left, right, preferred_element_type=F32)


def after(value, *others):
    return lax.optimization_barrier((value,) + others)[0]


def swap(value, axis, size, mask, *until):
    got = lax.ppermute(value, axis, [(i, i ^ mask) for i in range(size)])
    return after(got, *until) if until else got


def bits_of(size):
    return size.bit_length() - 1


def gather_later(value, size, *until):
    blocks = value[None]
    for bit in list(range(1, bits_of(size))) + [0]:
        mask = 1 << bit
        if bit == 0:
            pairs = [(i, i ^ 1) for i in range(size)]
        else:
            pairs = [(i, i ^ mask) for i in range(size) if i & mask]
        got = after(lax.ppermute(blocks, "grp", pairs), until[0] if bit else until[1])
        blocks = jnp.concatenate([blocks, got], axis=0)
    return blocks


def block_place(block, me, size):
    near = block ^ me
    return (near >> 1) | ((near & 1) << (bits_of(size) - 1))


def far_rows(weight, rep, size, reps, spread, before, y_until, x_until):
    rows = weight.shape[0]
    side = rep & 1
    half = rows // 2
    spread = spread and half % 16 == 0
    pieces = [(0, 0, weight)]
    for bit in range(1, bits_of(size)):
        mask = 1 << bit
        found = []
        for near, first, piece in pieces:
            if spread and near == 0:
                part = lax.dynamic_slice_in_dim(piece, side * half, half, 0)
                got = swap(after(part, *before), "grp", size, mask, *y_until)
                found.append((near | mask, side * half, got))
                found.append((near | mask, (1 - side) * half, swap(got, "rep", reps, 1, *x_until)))
            else:
                found.append((near | mask, first, swap(after(piece, *before), "grp", size, mask, *y_until)))
        pieces = pieces + found
    return pieces


def both_cores(pieces, own_other, size, me, rows, until=()):
    starts, found = [], []
    for near, first, piece in pieces:
        starts += [(me ^ near) * rows + first, (me ^ near ^ 1) * rows + first]
        other = own_other if near == 0 else swap(piece, "grp", size, 1, *until)
        found += [piece, other]
    return starts, found


def place_kernel(counts, starts, *refs):
    pieces, (out, sem) = refs[:-2], refs[-2:]
    copies = []
    for i, count in enumerate(counts):
        start = pl.multiple_of(starts[i] * 16, 16)
        copies.append(pltpu.make_async_copy(pieces[i], out.at[pl.ds(start, count), :], sem.at[i]))
    for copy in copies:
        copy.start()
    for copy in copies:
        copy.wait()


def place_rows(weight, size, starts, pieces):
    rows, columns = weight.shape
    counts = [piece.shape[0] for piece in pieces]
    anywhere = pl.BlockSpec(memory_space=pl.ANY)
    return pl.pallas_call(
        functools.partial(place_kernel, counts),
        grid_spec=pltpu.PrefetchScalarGridSpec(
            num_scalar_prefetch=1,
            grid=(1,),
            in_specs=[anywhere] * len(pieces),
            out_specs=pl.BlockSpec((size * rows, columns), lambda i, starts: (0, 0)),
            scratch_shapes=[pltpu.SemaphoreType.DMA((len(pieces),))],
        ),
        out_shape=jax.ShapeDtypeStruct((size * rows, columns), weight.dtype),
        compiler_params=pltpu.CompilerParams(vmem_limit_bytes=40 * 1024 * 1024),
        cost_estimate=pl.CostEstimate(
            flops=0, bytes_accessed=4 * size * rows * columns, transcendentals=0
        ),
    )(jnp.stack(starts).astype(jnp.int32) // 16, *pieces)


def by_core(left, me, size):
    rows = left.shape[1] // size
    core = me & 1
    if rows % 128 == 0:
        return [
            jnp.concatenate(
                [lax.dynamic_slice_in_dim(left, (2 * i + which) * rows, rows, 1) for i in range(size // 2)], axis=1
            )
            for which in (1 - core, core)
        ]
    strips = [left[:, i * rows : (i + 1) * rows] for i in range(size)]
    even = jnp.concatenate(strips[0::2], axis=1)
    odd = jnp.concatenate(strips[1::2], axis=1)
    return jnp.where(core == 0, odd, even), jnp.where(core == 0, even, odd)


def group_step(part, bit, me):
    size_left, rows, columns = part.shape
    split = part.reshape(2, size_left // 2, rows, columns)
    side = (me >> bit) & 1
    send = lax.dynamic_index_in_dim(split, 1 - side, 0, keepdims=False)
    keep = lax.dynamic_index_in_dim(split, side, 0, keepdims=False)
    return send, keep


def group_sum(part, me, size, *until):
    for bit in range(bits_of(part.shape[0]), 0, -1):
        send, keep = group_step(part, bit, me)
        part = add_low(keep, swap(send, "grp", size, 1 << bit, *until))
    return part


def add_low(keep, got):
    return (keep.astype(F32) + got.astype(F32)).astype(BF16)


def rep_halves(part, rep):
    axis = part.ndim - 2
    half = part.shape[axis] // 2
    side = rep & 1
    send = lax.dynamic_slice_in_dim(part, (1 - side) * half, half, axis)
    keep = lax.dynamic_slice_in_dim(part, side * half, half, axis)
    return send, keep


def scatter_far(part, rep, reps, *until):
    count = reps // 2
    place = rep >> 1
    pieces = part.reshape(count, -1, part.shape[1])
    total = lax.dynamic_index_in_dim(pieces, place, 0, keepdims=False).astype(F32)
    for mask in range(1, count):
        send = lax.dynamic_index_in_dim(pieces, place ^ mask, 0, keepdims=False)
        total = total + swap(send, "rep", reps, mask << 1, *until).astype(F32)
    return total.astype(BF16)


def share_far(own, rep, reps, *until):
    count = reps // 2
    place = rep >> 1
    near = [own] + [swap(own, "rep", reps, mask << 1, *until) for mask in range(1, count)]
    ordered = []
    for i in range(count):
        value = near[i]
        for j in range(1, count):
            value = jnp.where(place == j, near[i ^ j], value)
        ordered.append(value)
    return jnp.concatenate(ordered, axis=0)


def as_rows(part):
    return jnp.concatenate([part[:, i : i + D] for i in range(0, part.shape[1], D)], axis=0)


def in_order(own, got, rep):
    side = rep & 1
    low, high = jnp.where(side == 0, own, got), jnp.where(side == 0, got, own)
    return jnp.concatenate([low, high], axis=0)


def total_vector(value, size, reps, pace):
    steps = [("grp", bit) for bit in range(bits_of(size))] + [("rep", bit) for bit in range(bits_of(reps))]
    for i, (axis, bit) in enumerate(steps):
        count = size if axis == "grp" else reps
        value = value + swap(value, axis, count, 1 << bit, pace[min(i, len(pace) - 1)])
    return value


def other_grad(left, right):
    return token_product(left, right).astype(BF16)


def core_grad(theirs, left, right, size, *until):
    got = swap(theirs, "grp", size, 1, *until).astype(F32)
    part = (token_product(left, right) + got).astype(BF16)
    return part.reshape(size // 2, -1, part.shape[1])


def dot_nt(left, right):
    return lax.dot_general(left, right, (((1,), (1,)), ((), ())), preferred_element_type=F32)


def dot_nn(left, right):
    return lax.dot_general(left, right, (((1,), (0,)), ((), ())), preferred_element_type=F32)


def one_head(pair, head):
    lane = lax.broadcasted_iota(jnp.int32, pair.shape, 1)
    inside = (lane < HD) if head == 0 else (lane >= HD)
    return jnp.where(inside, pair, jnp.zeros_like(pair))


def per_head(first, second, shape):
    lane = lax.broadcasted_iota(jnp.int32, shape, 1)
    return jnp.where(lane < HD, first, second)


def start_of(block, me, size, count):
    return pl.multiple_of(block_place(block, me, size) * count, count)


def query_mask(info, qseg, kseg, bias, tile, count):
    me = info[0]
    for q in range(count // tile):
        rows = pl.ds(q * tile, tile)

        def fill(block, _):
            columns = pl.ds(pl.multiple_of(block * count, count), count)
            q_pos = me * count + q * tile + lax.broadcasted_iota(jnp.int32, (tile, count), 0)
            k_pos = block * count + lax.broadcasted_iota(jnp.int32, (tile, count), 1)
            seen = (k_pos <= q_pos) & (qseg[rows, 0:1] == kseg[0:1, columns])
            bias[rows, columns] = jnp.where(seen, 0.0, NEG)
            return 0

        lax.fori_loop(info[1 + q], me + 1, fill, 0)


def attend_kernel(size, tile, skip, info, q_ref, k_ref, v_ref, qseg, kseg, *refs):
    out, out_low, lse, lse_row, bias = refs[skip:]
    count = q_ref.shape[0]
    me = info[0]

    @pl.when(pl.program_id(0) == 0)
    def _():
        query_mask(info, qseg, kseg, bias, tile, count)

    for q in range(count // tile):
        rows = pl.ds(q * tile, tile)
        queries = q_ref[rows, :] * jnp.asarray(SCALE, BF16)

        def step(block, carry):
            tops, sums, total = carry
            start = start_of(block, me, size, count)
            keys = k_ref[pl.ds(start, count), :]
            values = v_ref[pl.ds(start, count), :]
            add = bias[rows, pl.ds(pl.multiple_of(block * count, count), count)]
            new_tops, new_sums, shrinks = [], [], []
            gain = jnp.zeros((tile, LANES), F32)
            for head in range(2):
                scores = dot_nt(queries, one_head(keys, head)) + add
                top = jnp.maximum(tops[head], jnp.max(scores, axis=1, keepdims=True))
                weights = jnp.exp(scores - top)
                shrink = jnp.exp(tops[head] - top)
                new_tops.append(top)
                shrinks.append(shrink)
                new_sums.append(sums[head] * shrink + jnp.sum(weights, axis=1, keepdims=True))
                gain = gain + dot_nn(weights.astype(BF16), one_head(values, head))
            total = total * per_head(shrinks[0], shrinks[1], total.shape) + gain
            return (tuple(new_tops), tuple(new_sums), total)

        column = jnp.zeros((tile, 1), F32)
        tops, sums, total = lax.fori_loop(
            info[1 + q],
            me + 1,
            step,
            ((column + NEG, column + NEG), (column, column), jnp.zeros((tile, LANES), F32)),
        )
        shape = (tile, LANES)
        result = total / per_head(sums[0], sums[1], shape)
        log_total = per_head(tops[0] + jnp.log(sums[0]), tops[1] + jnp.log(sums[1]), shape)
        out[rows, :] = result
        out_low[rows, :] = result.astype(BF16)
        lse[rows, :] = log_total
        turned = log_total.T
        lse_row[0, :, rows] = jnp.zeros((8, tile), F32)
        lse_row[0, 0:1, rows] = turned[0:1, :]
        lse_row[0, 1:2, rows] = turned[HD : HD + 1, :]


def query_grad_kernel(size, tile, info, q_ref, k_ref, v_ref, dout, out, lse, qseg, kseg, dq, bias):
    count = q_ref.shape[0]
    me = info[0]

    @pl.when(pl.program_id(0) == 0)
    def _():
        query_mask(info, qseg, kseg, bias, tile, count)

    for q in range(count // tile):
        rows = pl.ds(q * tile, tile)
        queries = q_ref[rows, :] * jnp.asarray(SCALE, BF16)
        douts = dout[rows, :]
        both = douts.astype(F32) * out[rows, :]
        deltas = [jnp.sum(one_head(both, head), axis=1, keepdims=True) for head in range(2)]
        logs = [lse[rows, 0:1], lse[rows, HD : HD + 1]]

        def step(block, total):
            start = start_of(block, me, size, count)
            keys = k_ref[pl.ds(start, count), :]
            values = v_ref[pl.ds(start, count), :]
            add = bias[rows, pl.ds(pl.multiple_of(block * count, count), count)]
            for head in range(2):
                one_keys = one_head(keys, head)
                scores = dot_nt(queries, one_keys) + add
                probs = jnp.exp(scores - logs[head])
                prob_grad = dot_nt(douts, one_head(values, head))
                score_grad = (probs * (prob_grad - deltas[head])).astype(BF16)
                total = total + dot_nn(score_grad, one_keys)
            return total

        total = lax.fori_loop(info[1 + q], me + 1, step, jnp.zeros((tile, LANES), F32))
        dq[rows, :] = (total * SCALE).astype(BF16)


def key_grad_kernel(
    size, tile, info, k_ref, v_ref, q_ref, dout, stats, kseg, qseg, dkv, bias
):
    count = k_ref.shape[0]
    me = info[0]
    first = 1 + count // tile

    @pl.when(pl.program_id(0) == 0)
    def _():
        for k in range(count // tile):
            rows = pl.ds(k * tile, tile)

            def fill(block, _):
                columns = pl.ds(pl.multiple_of(block * count, count), count)
                k_pos = me * count + k * tile + lax.broadcasted_iota(jnp.int32, (tile, count), 0)
                q_pos = block * count + lax.broadcasted_iota(jnp.int32, (tile, count), 1)
                seen = (k_pos <= q_pos) & (kseg[rows, 0:1] == qseg[0:1, columns])
                bias[rows, columns] = jnp.where(seen, 0.0, NEG)
                return 0

            lax.fori_loop(me, info[first + k], fill, 0)

    for k in range(count // tile):
        rows = pl.ds(k * tile, tile)
        keys = k_ref[rows, :]
        values = v_ref[rows, :]

        def step(block, carry):
            key_total, value_total = carry
            place = block_place(block, me, size)
            start = pl.multiple_of(place * count, count)
            queries = q_ref[pl.ds(start, count), :] * jnp.asarray(SCALE, BF16)
            douts = dout[pl.ds(start, count), :]
            add = bias[rows, pl.ds(pl.multiple_of(block * count, count), count)]
            for head in range(2):
                one_queries = one_head(queries, head)
                one_douts = one_head(douts, head)
                scores = dot_nt(keys, one_queries) + add
                probs = jnp.exp(scores - stats[place, 0, head : head + 1, :])
                prob_grad = dot_nt(values, one_douts)
                score_grad = probs * (prob_grad - stats[place, 0, 2 + head : 3 + head, :])
                value_total = value_total + dot_nn(probs.astype(BF16), one_douts)
                key_total = key_total + dot_nn(score_grad.astype(BF16), one_queries)
            return (key_total, value_total)

        empty = jnp.zeros((tile, LANES), F32)
        key_total, value_total = lax.fori_loop(me, info[first + k], step, (empty, empty))
        dkv[rows, :LANES] = key_total.astype(BF16)
        dkv[rows, LANES:] = value_total.astype(BF16)


def strip(rows, first, stride=1):
    return pl.BlockSpec((rows, LANES), lambda p, info: (0, first + stride * p))


def whole(shape):
    return pl.BlockSpec(shape, lambda p, info: (0,) * len(shape))


def paired(count, blocks, first=0):
    if blocks is None:
        return pl.BlockSpec((1, 8, count), lambda p, info: (first + p, 0, 0))
    return pl.BlockSpec((blocks, 1, 8, count), lambda p, info: (0, first + p, 0, 0))


def call(body, in_specs, out_specs, out_shape, count, seq_len, products, pairs, mib=60, aliases=None):
    return pl.pallas_call(
        body,
        grid_spec=pltpu.PrefetchScalarGridSpec(
            num_scalar_prefetch=1,
            grid=(pairs,),
            in_specs=in_specs,
            out_specs=out_specs,
            scratch_shapes=[pltpu.VMEM((count, seq_len), F32)],
        ),
        out_shape=out_shape,
        input_output_aliases=aliases or {},
        compiler_params=pltpu.CompilerParams(vmem_limit_bytes=mib * 1024 * 1024),
        cost_estimate=pl.CostEstimate(
            flops=products * 2 * count * count * 2 * 256 * 2 * pairs,
            bytes_accessed=8 * 1024 * 1024,
            transcendentals=count * count * 4 * pairs,
        ),
    )


def key_value_strips(rows, first):
    return [strip(rows, PAIRS + 2 * first, 2), strip(rows, PAIRS + 2 * first + 1, 2)]


def attend(first, pairs, info, qkv_all, earlier, seg_col, seg_row, count, seq_len, size, tile):
    out = jax.ShapeDtypeStruct((count, D), F32)
    return call(
        functools.partial(attend_kernel, size, tile, len(earlier)),
        [strip(count, first)]
        + key_value_strips(seq_len, first)
        + [whole((count, 128)), whole((1, seq_len))]
        + [pl.BlockSpec(memory_space=pl.ANY)] * len(earlier),
        [strip(count, first), strip(count, first), strip(count, first), paired(count, None, first)],
        [out, jax.ShapeDtypeStruct((count, D), BF16), out, jax.ShapeDtypeStruct((PAIRS, 8, count), F32)],
        count,
        seq_len,
        2,
        pairs,
        40,
        {6 + i: i for i in range(len(earlier))},
    )(info, qkv_all, qkv_all, qkv_all, seg_col, seg_row, *earlier)


def query_grads(first, pairs, info, qkv_all, dout, out, lse, seg_col, seg_row, count, seq_len, size, tile):
    return call(
        functools.partial(query_grad_kernel, size, tile),
        [strip(count, first)] + key_value_strips(seq_len, first)
        + [strip(count, first)] * 3
        + [whole((count, 128)), whole((1, seq_len))],
        strip(count, 0),
        jax.ShapeDtypeStruct((count, pairs * LANES), BF16),
        count,
        seq_len,
        3,
        pairs,
    )(info, qkv_all, qkv_all, qkv_all, dout, out, lse, seg_col, seg_row)


def key_grads(first, pairs, info, qkv_all, dout_all, stats, seg_col, seg_row, count, seq_len, size, tile):
    return call(
        functools.partial(key_grad_kernel, size, tile),
        key_value_strips(count, first) + [strip(seq_len, first)] * 2
        + [paired(count, size, first)]
        + [whole((count, 128)), whole((1, seq_len))],
        pl.BlockSpec((count, 2 * LANES), lambda p, info: (0, p)),
        jax.ShapeDtypeStruct((count, pairs * 2 * LANES), BF16),
        count,
        seq_len,
        4,
        pairs,
    )(info, qkv_all, qkv_all, qkv_all, dout_all, stats, seg_col, seg_row)


def key_value_mixed(columns):
    rows = columns.shape[0]
    pairs = columns.reshape(rows, 2, PAIRS, LANES)
    return jnp.concatenate([pairs[:, i % 2, i // 2] for i in range(2 * PAIRS)], axis=1)


def key_value_apart(columns):
    rows, width = columns.shape
    strips = [columns[:, i * LANES : (i + 1) * LANES] for i in range(width // LANES)]
    return strips[0::2], strips[1::2]


def per_device(
    reps,
    size,
    tokens,
    segment_ids,
    w_qkv,
    w_out,
    w_up,
    w_down,
    norm_gains,
    norm_shifts,
    proj_biases,
    up_bias,
    cotangent,
):
    count = tokens.shape[1]
    seq_len = segment_ids.shape[1]
    tile = min(512, count)
    me = lax.axis_index("grp")
    rep = lax.axis_index("rep")
    seg_row = segment_ids[0]
    first_row = me * count
    own_seg = lax.dynamic_slice_in_dim(seg_row, first_row, count, 0)
    seg_col = jnp.broadcast_to(own_seg[:, None], (count, 128))
    starts = own_seg[0::tile]
    ends = own_seg[tile - 1 :: tile]
    low = jnp.sum((seg_row[None, :] < starts[:, None]).astype(jnp.int32), axis=1) // count
    high = (jnp.sum((seg_row[None, :] <= ends[:, None]).astype(jnp.int32), axis=1) - 1) // count + 1
    info = jnp.concatenate([me[None].astype(jnp.int32), low, high])
    seg_row = seg_row[None]

    mixed_qkv = jnp.concatenate([w_qkv[:, :D], key_value_mixed(w_qkv[:, D:])], axis=1)
    near_qkv = far_rows(mixed_qkv, rep, size, reps, True, (), (), ())
    first_far, last_far = near_qkv[1][2], near_qkv[-1][2]
    starts_qkv, pieces_qkv = both_cores(near_qkv, swap(mixed_qkv, "grp", size, 1), size, me, w_qkv.shape[0])
    other_out, other_up, other_down = [swap(weight, "grp", size, 1) for weight in (w_out, w_up, w_down)]
    qkv_full = place_rows(w_qkv, size, starts_qkv, pieces_qkv)

    source = tokens[0].astype(F32)
    normed = layer_norm(source, norm_gains[0], norm_shifts[0]).astype(BF16)
    normed_all = after(normed, first_far)[None]
    far_tokens = None
    for bit in list(range(1, bits_of(size))) + [0]:
        got = swap(normed_all, "grp", size, 1 << bit)
        if bit:
            far_tokens = got = after(got, last_far)
        normed_all = jnp.concatenate([normed_all, got], axis=0)
    normed_all = normed_all.reshape(seq_len, D)
    value_bias = proj_biases[1].reshape(PAIRS, LANES)
    bias = jnp.stack([jnp.zeros_like(value_bias), value_bias], axis=1).reshape(-1)
    shift = jnp.concatenate([proj_biases[0], bias])
    qkv_all = (add_rows(normed_all, qkv_full) + shift).astype(BF16)
    heads = (info, after(qkv_all, other_out, other_up, other_down))
    shapes = (seg_col, seg_row, count, seq_len, size, tile)
    part = PAIRS // 2
    earlier = attend(0, part, *heads, (), *shapes)
    near_up = far_rows(w_up, rep, size, reps, True, (far_tokens,), earlier, ())
    near_out = far_rows(w_out, rep, size, reps, False, (far_tokens,), earlier, ())
    earlier = [after(value, near_up[1][2], near_out[1][2]) for value in earlier]
    attended_f, attended, lse, lse_row = attend(part, part, *heads, earlier, *shapes)
    near_up = [(near, first, after(piece, attended)) for near, first, piece in near_up]
    near_down = far_rows(w_down, rep, size, reps, True, (near_up[1][2],), (attended,), ())
    starts_out, pieces_out = both_cores(near_out, other_out, size, me, w_out.shape[0], (attended,))
    starts_up, pieces_up = both_cores(near_up, other_up, size, me, w_up.shape[0])
    out_full = place_rows(w_out, size, starts_out, pieces_out)
    middle = source + add_rows(attended, out_full) + proj_biases[2]
    up_full = place_rows(w_up, size, starts_up, pieces_up)
    second = layer_norm(middle, norm_gains[1], norm_shifts[1]).astype(BF16)
    hidden_pre = add_rows(second, up_full) + up_bias
    hidden = jax.nn.gelu(hidden_pre).astype(BF16)
    upstream = cotangent[0]
    upstream_f = upstream.astype(F32)
    hidden_theirs, hidden_mine = by_core(hidden, me, size)
    down_theirs = other_grad(hidden_theirs, upstream)
    near_down = [(near, first, after(piece, hidden)) for near, first, piece in near_down]
    starts_down, pieces_down = both_cores(near_down, other_down, size, me, w_down.shape[0], (down_theirs,))
    down_full = place_rows(w_down, size, starts_down, pieces_down)
    hidden_grad = back_rows(after(upstream, down_theirs), down_full)
    _, gelu_pull = jax.vjp(jax.nn.gelu, hidden_pre)
    pre_grad = gelu_pull(hidden_grad)[0].astype(BF16)
    second_theirs, second_mine = by_core(second, me, size)
    up_theirs = other_grad(second_theirs, pre_grad)
    down_part = core_grad(down_theirs, after(hidden_mine, up_theirs), upstream, size, pre_grad)
    down_send, down_keep = group_step(down_part, bits_of(size) - 1, me)

    up_part = core_grad(up_theirs, second_mine, after(pre_grad, down_send), size, down_send)
    up_send, up_keep = rep_halves(up_part, rep)

    second_grad = back_rows(after(pre_grad, up_send), up_full)
    _, second_pull = jax.vjp(layer_norm, middle, norm_gains[1], norm_shifts[1])
    middle_part, gain_second, shift_second = second_pull(second_grad)
    middle_grad = upstream_f + middle_part
    branch_grad = middle_grad.astype(BF16)
    dout = back_rows(branch_grad, out_full).astype(BF16)
    row = lax.broadcasted_iota(jnp.int32, (8 * PAIRS, D), 0)
    minor = row % 8 - 2
    lane_head = lax.broadcasted_iota(jnp.int32, (8 * PAIRS, D), 1) // HD
    picks = ((row // 8 * 2 + minor == lane_head) & (minor >= 0) & (minor < 2)).astype(F32)
    delta_row = jnp.einsum(
        "ed,td->et", picks, dout.astype(F32) * attended_f, precision=lax.Precision.HIGHEST
    ).reshape(PAIRS, 8, count)

    attended_theirs, attended_mine = by_core(attended, me, size)
    normed_theirs, normed_mine = by_core(normed, me, size)
    out_theirs = other_grad(attended_theirs, after(branch_grad, dout))
    queries_one = query_grads(0, part, *heads, after(dout, up_send, out_theirs, delta_row), attended_f, lse, *shapes)

    out_part = core_grad(out_theirs, attended_mine, after(branch_grad, queries_one), size, queries_one)
    down_part = add_low(down_keep, swap(down_send, "grp", size, size // 2, queries_one))
    down_send, down_keep = rep_halves(group_sum(down_part, me, size)[0], rep)
    up_part = add_low(up_keep, swap(up_send, "rep", reps, 1, queries_one))
    up_send, up_keep = group_step(up_part, bits_of(size) - 1, me)
    queries_two = query_grads(part, part, *heads, after(dout, up_send, down_send, out_part), attended_f, lse, *shapes)
    down_part = add_low(down_keep, swap(down_send, "rep", reps, 1, queries_two))
    up_part = add_low(up_keep, swap(up_send, "grp", size, size // 2, queries_two))
    up_part = group_sum(up_part, me, size)[0]
    both_part = jnp.concatenate([down_part, as_rows(up_part)], axis=0)
    stats = gather_later(lse_row + delta_row, size, queries_one, queries_two)
    dout_all = gather_later(dout, size, queries_one, queries_two).reshape(seq_len, D)

    both_queries = jnp.concatenate([queries_one, queries_two], axis=1)
    query_theirs = other_grad(normed_theirs, both_queries)
    mixed_one = key_grads(0, part, *heads, after(dout_all, query_theirs, both_part, stats), stats, *shapes)

    query_part = core_grad(query_theirs, normed_mine, after(both_queries, mixed_one), size, mixed_one)
    pair_part = jnp.concatenate([query_part, out_part], axis=1)
    pair_send, pair_keep = group_step(pair_part, bits_of(size) - 1, me)
    one_theirs = other_grad(normed_theirs, mixed_one)
    both_part = scatter_far(both_part, rep, reps, mixed_one)
    mixed_two = key_grads(
        part, part, *heads, after(dout_all, one_theirs, pair_send, both_part), stats, *shapes
    )

    two_theirs = other_grad(normed_theirs, mixed_two)
    joined_grad = jnp.concatenate([both_queries, mixed_one, mixed_two], axis=1)
    normed_grad = back_rows(after(joined_grad, two_theirs), qkv_full)
    _, first_pull = jax.vjp(layer_norm, source, norm_gains[0], norm_shifts[0])
    source_part, gain_first, shift_first = first_pull(normed_grad)
    input_grad = middle_grad + source_part
    one_part = core_grad(one_theirs, normed_mine, after(mixed_one, mixed_two), size, mixed_two)
    pair_part = add_low(pair_keep, swap(pair_send, "grp", size, size // 2, mixed_two))
    pair_part = group_sum(pair_part, me, size)[0]
    one_part = group_sum(one_part, me, size, gain_first)[0]
    both_every = share_far(both_part, rep, reps, mixed_two)
    pair_send, pair_keep = rep_halves(pair_part, rep)
    pair_part = add_low(pair_keep, swap(pair_send, "rep", reps, 1, gain_first))

    two_part = core_grad(two_theirs, normed_mine, after(mixed_two, gain_first), size, gain_first)
    block_out = middle + add_rows(after(hidden, two_part), down_full) + proj_biases[3]
    block_out = block_out.astype(BF16)
    two_part = group_sum(two_part, me, size, block_out)[0]
    pace = [two_part]
    mixed_send, mixed_keep = rep_halves(jnp.concatenate([one_part, two_part], axis=0), rep)
    mixed_part = add_low(mixed_keep, swap(mixed_send, "rep", reps, 1))
    pace.append(mixed_part)
    pair_part = scatter_far(after(pair_part, block_out), rep, reps, mixed_part)
    both_got = swap(both_every, "rep", reps, 1, mixed_part)
    mixed_part = scatter_far(mixed_part, rep, reps)
    pace.append(mixed_part)
    pair_every = share_far(pair_part, rep, reps, mixed_part)
    mixed_every = share_far(mixed_part, rep, reps)
    pace.append(mixed_every)
    pair_got = swap(pair_every, "rep", reps, 1, mixed_every)
    mixed_got = swap(mixed_every, "rep", reps, 1)

    rows = w_qkv.shape[0]
    tall = w_down.shape[0] // 2
    grad_down = in_order(both_every[:tall], both_got[:tall], rep)
    wide = [
        in_order(both_every[i : i + rows // 2], both_got[i : i + rows // 2], rep)
        for i in range(tall, both_every.shape[0], rows // 2)
    ]
    grad_up = jnp.concatenate(wide, axis=1)
    pair_grad = in_order(pair_every, pair_got, rep).astype(F32)
    mixed_grad = in_order(mixed_every, mixed_got, rep).astype(F32)
    one_keys, one_values = key_value_apart(mixed_grad[:rows])
    two_keys, two_values = key_value_apart(mixed_grad[rows:])
    grad_qkv = jnp.concatenate([pair_grad[:rows]] + one_keys + two_keys + one_values + two_values, axis=1)
    grad_out = pair_grad[rows:]

    joined_sum = jnp.sum(joined_grad.astype(F32), axis=0, keepdims=True)
    value_sum = joined_sum[:, D:].reshape(PAIRS, 2, LANES)[:, 1].reshape(1, D)
    vectors = jnp.concatenate(
        [
            gain_first[None],
            gain_second[None],
            shift_first[None],
            shift_second[None],
            joined_sum[:, :D],
            value_sum,
            jnp.sum(branch_grad.astype(F32), axis=0, keepdims=True),
            jnp.sum(upstream_f, axis=0, keepdims=True),
            jnp.sum(pre_grad.astype(F32), axis=0).reshape(FF // D, D),
        ],
        axis=0,
    )
    vectors = total_vector(vectors, size, reps, pace)
    return (
        block_out[None],
        input_grad[None],
        grad_qkv,
        grad_out,
        grad_up.astype(F32),
        grad_down.astype(F32),
        vectors[:2],
        vectors[2:4],
        vectors[4:8],
        vectors[8:].reshape(-1),
    )


def solution(mesh):
    return jax.shard_map(
        functools.partial(per_device, mesh.shape["rep"], mesh.shape["grp"]),
        mesh=mesh,
        in_specs=(
            P("rep", "grp", None),
            P("rep", None),
            P("grp", None),
            P("grp", None),
            P("grp", None),
            P("grp", None),
            P(),
            P(),
            P(),
            P(),
            P("rep", "grp", None),
        ),
        out_specs=(
            P("rep", "grp", None),
            P("rep", "grp", None),
            P("grp", None),
            P("grp", None),
            P("grp", None),
            P("grp", None),
            P(),
            P(),
            P(),
            P(),
        ),
        check_vma=False,
    )
```

time: 487 us -> 416 us (0.85)
  waiting for transfers between devices: 166 us -> 112 us
  local copies, waits for them, and re-layouts: 64.2 us -> 26.7 us
  other arithmetic: 38.3 us -> 54.5 us
  Pallas kernels: 48.3 us -> 60.8 us
  matrix products: 64.6 us -> 53.7 us
    ppermute x47 -> x61, waiting for transfers between devices: 162 us -> 93.9 us  [swap(): got = lax.ppermute(value, axis, [(i, i ^ mask) for i in range(size)])]
    dynamic_update_slice x22 -> x0, local copies, waits for them, and re-layouts: 18.7 us -> none  [the longest x11 10.2 us: gather_weight(): lax.dynamic_update_slice(whole, other, ((me ^ near ^ 1) * rows + first, 0))]
    ppermute x4, waiting for transfers between devices: 4.05 us -> 17.7 us  [gather_later(): lax.ppermute(blocks, 'grp', pairs)]
    pallas_call x3 -> x8, Pallas kernels: 33.6 us -> 45.2 us  [the longest x2 24.3 us: key_grads(): call(functools.partial(key_grad_kernel, size, tile), key_value_strips(cou...]
    concatenate x17 -> x14, other arithmetic: 6.51 us -> 17.2 us  [the longest x4 8.5 us: gather_later(): blocks = jnp.concatenate([blocks, got], axis=0)]
    all_to_all x2 -> x0, starting transfers between devices: 10.1 us -> none  [the longest x1 5.34 us: spread_last(): lax.all_to_all(jnp.broadcast_to(own[None], pieces.shape), 'rep', 0, 0, ti...]
    unnamed x155 -> x237, local copies, waits for them, and re-layouts: 19.7 us -> 11 us
    convert_element_type x9 -> x14, other arithmetic: 6.62 us -> 14.8 us  [the longest x6 8.91 us: core_grad(): part = (token_product(left, right) + got).astype(BF16)]
  transfers between devices with their start and end apart: 53 -> 65, of which waited for: 18 -> 20; matrix products, arithmetic and copies ran while one was open for 30% -> 28% of each run, Pallas kernels for 10% -> 12%
where the time goes in v1:
time: 416 us; the launch traced here: 410 us
  waiting for transfers between devices  112 us (27%)
  starting transfers between devices  96.6 us (23%)
  Pallas kernels  60.8 us (15%)
  other arithmetic  54.5 us (13%)
  matrix products  53.7 us (13%)
  local copies, waits for them, and re-layouts  26.7 us (6%)
  between operations  6.31 us (2%)
    ppermute x61, waiting for transfers between devices, swap(): got = lax.ppermute(value, axis, [(i, i ^ mask) for i in range(size)])  93.9 us
    ppermute x61, starting transfers between devices, swap(): got = lax.ppermute(value, axis, [(i, i ^ mask) for i in range(size)])  93.2 us
    pallas_call x2, Pallas kernels, key_grads(): call(functools.partial(key_grad_kernel, size, tile), key_value_strips(cou...  24.3 us
    dot_general x12, matrix products, token_product(): return jnp.einsum('tc,te->ce', left, right, preferred_element_type=F32)  19.3 us
    dot_general x4, matrix products, add_rows(): return jnp.dot(left, piece, preferred_element_type=F32)  18.4 us
    ppermute x4, waiting for transfers between devices, gather_later(): lax.ppermute(blocks, 'grp', pairs)  17.7 us
    pallas_call x2, Pallas kernels, query_grads(): call(functools.partial(query_grad_kernel, size, tile), [strip(count, firs...  15.5 us
    dot_general x4, matrix products, back_rows(): return jnp.einsum('te,ce->tc', right, piece, preferred_element_type=F32)  13.8 us
  transfers between devices with their start and end apart: 65, of which 20 were waited for; matrix products, arithmetic and copies ran while one was open for 28% of the time, Pallas kernels for 12%

profile of v1, /device:TPU:0, one launch (start us, length us, event | category | flops | bytes accessed | tf_op | source)
XLA Modules:
  0.0 410.1 jit_solution(12381136859086239147)
XLA Ops:
  4.4 2.6 collective-permute-start
  8.9 8.9 %collective-permute-done.refs_2_ = bf16[96,2304]{1,0:T(8,128)(2,1)S(1)} collective-permute-done((bf16[96,2304]{1,0:T(8,128)(2,1)S(1)}, bf16[96,2304]{1,0:T(8,128)(2,1)S(1)}, u32[]{:S(2)}, u32[]{:S(2)}) %collective-permute-start) | collective-permute-done | bytes 442400 | tf_op jit(solution)/shard_map/ppermute | solution.py:46
  17.8 1.7 collective-permute-start.1
  21.1 2.0 fusion.83
  23.1 8.0 %collective-permute-done.2.refs_4_ = bf16[96,2304]{1,0:T(8,128)(2,1)S(1)} collective-permute-done((bf16[96,2304]{1,0:T(8,128)(2,1)S(1)}, bf16[96,2304]{1,0:T(8,128)(2,1)S(1)}, u32[]{:S(2)}, u32[]{:S(2)}) %collective-permute-start.2) | collective-permute-done | bytes 442400 | tf_op jit(solution)/shard_map/ppermute | solution.py:46
  31.1 6.0 %collective-permute-done.1 = bf16[1,512,768]{2,1,0:T(8,128)(2,1)S(1)} collective-permute-done((bf16[1,512,768]{2,1,0:T(8,128)(2,1)S(1)}, bf16[1,512,768]{2,1,0:T(8,128)(2,1)S(1)}, u32[]{:S(2)}, u32[]{:S(2)}) %collective-permute-start.1) | collective-permute-done | bytes 786464 | tf_op jit(solution)/shard_map/ppermute | solution.py:46
  49.3 2.1 shard_map.186
  52.1 2.4 pad_maximum_fusion
  54.4 8.1 %add_convert_fusion.q_ref.k_ref.v_ref = bf16[2048,2304]{1,0:T(8,128)(2,1)S(1)} fusion(bf16[2048,768]{1,0:T(8,128)(2,1)S(1)} %bitcast.249, bf16[768,2304]{1,0:T(8,128)(2,1)S(1)} %shard_map.186, f32[2304]{0:T(1024)S(1)} %pad_maximum_fusion.27), kind=kOutput, calls=%fused_computation | convolution fusion | flops 7257194496 | bytes 16131072 | tf_op jit(solution)/shard_map/dot_general | solution.py:30
  62.7 6.7 %shard_map.187 = (f32[512,768]{1,0:T(8,128)S(1)}, bf16[512,768]{1,0:T(8,128)(2,1)S(1)}, f32[512,768]{1,0:T(8,128)S(1)}, f32[6,8,512]{2,1,0:T(8,128)S(1)}) custom-call(s32[3]{0:T(128)S(1)} %pad_add_fusion.info, bf16[2048,2304]{1,0:T(8,128)(2,1)S(1)} %add_convert_fusion.q_ref.k_ref.v_ref, bf16[2048,2304]{1,0:T(8,128)(2,1)S(1)} %add_convert_fusion.q_ref.k_ref.v_ref, ...), custom_call_target="tpu_custom_call" | custom-call | flops 3221225472 | bytes 8388608 | tf_op jit(solution)/shard_map/pallas_call | solution.py:449
  69.9 3.6 collective-permute-start.12
  73.6 6.7 %shard_map.188 = (f32[512,768]{1,0:T(8,128)S(1)}, bf16[512,768]{1,0:T(8,128)(2,1)S(1)}, f32[512,768]{1,0:T(8,128)S(1)}, f32[6,8,512]{2,1,0:T(8,128)S(1)}) custom-call(s32[3]{0:T(128)S(1)} %pad_add_fusion.info, bf16[2048,2304]{1,0:T(8,128)(2,1)S(1)} %add_convert_fusion.q_ref.k_ref.v_ref, ...), custom_call_target="tpu_custom_call", output_to_operand_aliasing={{0}: (6, {}), {1}: (7, {}), {2}: (8, {}), {3}: (9, {})} | custom-call | flops 3221225472 | bytes 8388608 | tf_op jit(solution)/shard_map/pallas_call | solution.py:449
  81.9 3.7 collective-permute-start.13
  85.6 16.1 %collective-permute-start.16 = (bf16[384,768]{1,0:T(8,128)(2,1)S(1)}, bf16[384,768]{1,0:T(8,128)(2,1)S(1)}, u32[]{:S(2)}, u32[]{:S(2)}) collective-permute-start(bf16[384,768]{1,0:T(8,128)(2,1)S(1)} %copy-done.84), channel_id=1, source_target_pairs={{0,2},{1,3},{2,0},{3,1},{4,6},{5,7},{6,4},{7,5},{8,10},{9,11},{10,... | collective-permute-start | bytes 1769480 | tf_op jit(solution)/shard_map/ppermute | solution.py:46
  102.8 1.6 shard_map.189
  106.9 8.3 %collective-permute-done.16.refs_2_ = bf16[384,768]{1,0:T(8,128)(2,1)S(1)} collective-permute-done((bf16[384,768]{1,0:T(8,128)(2,1)S(1)}, bf16[384,768]{1,0:T(8,128)(2,1)S(1)}, u32[]{:S(2)}, u32[]{:S(2)}) %collective-permute-start.16) | collective-permute-done | bytes 589856 | tf_op jit(solution)/shard_map/ppermute | solution.py:46
  115.6 2.2 shard_map.190
  117.8 4.0 multiply_convert_fusion
  122.0 7.9 %collective-permute-done.18.refs_4_ = bf16[384,768]{1,0:T(8,128)(2,1)S(1)} collective-permute-done((bf16[384,768]{1,0:T(8,128)(2,1)S(1)}, bf16[384,768]{1,0:T(8,128)(2,1)S(1)}, u32[]{:S(2)}, u32[]{:S(2)}) %collective-permute-start.18) | collective-permute-done | bytes 589856 | tf_op jit(solution)/shard_map/ppermute | solution.py:46
  130.3 2.8 convolution_convert_fusion.1
  137.4 7.0 %convert_reduce_fusion = (f32[3072]{0:T(1024)S(1)}, bf16[512,3072]{1,0:T(8,128)(2,1)S(1)}) fusion(f32[512,3072]{1,0:T(8,128)S(1)} %get-tuple-element.280, f32[3072]{0:T(1024)S(1)} %copy-done.100, bf16[512,768]{1,0:T(8,128)(2,1)S(1)} %bitcast.244, bf16[3072,768]{1,0:T(8,128)(2,1)S(1)} %shard_map.191), kind=kOutput, calls=%fused_computation.10 | convolution fusion | flops 2452091904 | bytes 14966784 | tf_op jit(solution)/shard_map/te,ce->tc/dot_general | solution.py:34
  144.4 3.0 convolution_convert_fusion
  147.4 3.2 fusion.95
  150.8 5.4 %add_convert_fusion.4 = bf16[512,768]{1,0:T(8,128)(2,1)} fusion(f32[512,768]{1,0:T(8,128)S(1)} %copy-done.28, bf16[512,3072]{1,0:T(8,128)(2,1)} %copy-done.50, bf16[3072,768]{1,0:T(8,128)(2,1)S(1)} %bitcast.234, f32[768]{0:T(1024)S(1)} %get-tuple-element.181), kind=kOutput, calls=%fused_computation.56 | convolution fusion | flops 2417098752 | bytes 10226688 | tf_op jit(solution)/shard_map/dot_general | solution.py:30
  156.2 2.6 add_convert_fusion.2
  163.6 2.6 add_convert_fusion.1
  167.9 3.0 multiply_reduce_fusion
  173.4 1.7 convolution_convert_fusion.2.dout
  178.1 2.2 fusion.29
  180.4 7.8 %shard_map.192 = bf16[512,384]{1,0:T(8,128)(2,1)} custom-call(s32[3]{0:T(128)} %copy-done.20, bf16[2048,2304]{1,0:T(8,128)(2,1)} %copy-done, bf16[2048,2304]{1,0:T(8,128)(2,1)} %copy-done, bf16[2048,2304]{1,0:T(8,128)(2,1)} %copy-done, bf16[512,768]{1,0:T(8,128)(2,1)} %convolution_convert_fusion.2.dout, f32[512,768]{1,0:T(8,128)} %copy-done.1, ...), custom_call_target="tpu_custom_call" | custom-call | flops 4831838208 | bytes 8388608 | tf_op jit(solution)/shard_map/pallas_call | solution.py:467
  190.4 17.7 %collective-permute-done.29 = f32[1,6,8,512]{3,2,1,0:T(8,128)S(1)} collective-permute-done((f32[1,6,8,512]{3,2,1,0:T(8,128)S(1)}, f32[1,6,8,512]{3,2,1,0:T(8,128)S(1)}, u32[]{:S(2)}, u32[]{:S(2)}) %collective-permute-start.29) | collective-permute-done | bytes 98336 | tf_op jit(solution)/shard_map/ppermute | solution.py:62
  208.2 1.6 fusion.7
  211.6 2.9 pad_maximum_fusion.5
  214.9 1.7 add_convert_fusion.3
  218.5 7.8 %shard_map.193 = bf16[512,384]{1,0:T(8,128)(2,1)} custom-call(s32[3]{0:T(128)} %copy-done.20, bf16[2048,2304]{1,0:T(8,128)(2,1)} %copy-done, bf16[2048,2304]{1,0:T(8,128)(2,1)} %copy-done, bf16[2048,2304]{1,0:T(8,128)(2,1)} %copy-done, bf16[512,768]{1,0:T(8,128)(2,1)} %convolution_convert_fusion.2.dout, f32[512,768]{1,0:T(8,128)} %copy-done.1, ...), custom_call_target="tpu_custom_call" | custom-call | flops 4831838208 | bytes 8388608 | tf_op jit(solution)/shard_map/pallas_call | solution.py:467
  226.3 2.5 convolution_convert_fusion.5
  228.8 3.7 collective-permute-start.31
  232.5 1.7 pad_maximum_fusion.15.stats
  239.6 4.4 %collective-permute-start.32 = (bf16[192,768]{1,0:T(8,128)(2,1)}, bf16[192,768]{1,0:T(8,128)(2,1)}, u32[]{:S(2)}, u32[]{:S(2)}) collective-permute-start(bf16[192,768]{1,0:T(8,128)(2,1)} %get-tuple-element.223), channel_id=1, source_target_pairs={{0,8},{4,12},{8,0},{12,4},{16,24},{20,28},{24,16},{28,20},{1,9},{5... | collective-permute-start | bytes 884744 | tf_op jit(solution)/shard_map/ppermute | solution.py:46
  244.0 3.9 pad_maximum_fusion.1
  247.9 12.2 %shard_map.194 = bf16[512,768]{1,0:T(8,128)(2,1)} custom-call(s32[3]{0:T(128)} %copy-done.20, bf16[2048,2304]{1,0:T(8,128)(2,1)} %copy-done, bf16[2048,2304]{1,0:T(8,128)(2,1)} %copy-done, bf16[2048,2304]{1,0:T(8,128)(2,1)} %copy-done, bf16[2048,768]{1,0:T(8,128)(2,1)} %bitcast.235, f32[4,6,8,512]{3,2,1,0:T(8,128)} %pad_maximum_fusion.15.stats, ...), custom_call_target="tpu_custom_call" | custom-call | flops 6442450944 | bytes 8388608 | tf_op jit(solution)/shard_map/pallas_call | solution.py:482
  264.2 2.1 fusion.42
  266.3 12.1 %shard_map.195 = bf16[512,768]{1,0:T(8,128)(2,1)} custom-call(s32[3]{0:T(128)} %copy-done.20, bf16[2048,2304]{1,0:T(8,128)(2,1)} %copy-done, bf16[2048,2304]{1,0:T(8,128)(2,1)} %copy-done, bf16[2048,2304]{1,0:T(8,128)(2,1)} %copy-done, bf16[2048,768]{1,0:T(8,128)(2,1)} %bitcast.236, f32[4,6,8,512]{3,2,1,0:T(8,128)} %pad_maximum_fusion.15.stats, ...), custom_call_target="tpu_custom_call" | custom-call | flops 6442450944 | bytes 8388608 | tf_op jit(solution)/shard_map/pallas_call | solution.py:482
  278.4 2.0 convert_reduce_fusion.1
  281.8 2.1 collective-permute-start.35
  285.3 2.9 collective-permute-start.56
  288.2 2.1 fusion.101
  291.8 1.8 add_bitcast_fusion
  296.1 15.9 %collective-permute-done.58 = bf16[192,768]{1,0:T(8,128)(2,1)} collective-permute-done((bf16[192,768]{1,0:T(8,128)(2,1)}, bf16[192,768]{1,0:T(8,128)(2,1)}, u32[]{:S(2)}, u32[]{:S(2)}) %collective-permute-start.58) | collective-permute-done | bytes 294944 | tf_op jit(solution)/shard_map/ppermute | solution.py:46
  314.6 11.7 %collective-permute-start.36 = (bf16[192,768]{1,0:T(8,128)(2,1)S(1)}, bf16[192,768]{1,0:T(8,128)(2,1)S(1)}, u32[]{:S(2)}, u32[]{:S(2)}) collective-permute-start(bf16[192,768]{1,0:T(8,128)(2,1)S(1)} %dynamic-slice_bitcast_fusion.4), channel_id=1, source_target_pairs={{0,4},{4,0},{8,12},{12,8},{16,20},{20,16},{24,28},{28,24},{1,5},{5... | collective-permute-start | bytes 884744 | tf_op jit(solution)/shard_map/ppermute | solution.py:46
  327.5 2.1 collective-permute-start.39
  330.0 4.1 %collective-permute-done.36 = bf16[192,768]{1,0:T(8,128)(2,1)S(1)} collective-permute-done((bf16[192,768]{1,0:T(8,128)(2,1)S(1)}, bf16[192,768]{1,0:T(8,128)(2,1)S(1)}, u32[]{:S(2)}, u32[]{:S(2)}) %collective-permute-start.36) | collective-permute-done | bytes 294944 | tf_op jit(solution)/shard_map/ppermute | solution.py:46
  334.2 3.2 collective-permute-done.39
  337.5 5.9 %collective-permute-done.41 = bf16[1,192,768]{2,1,0:T(8,128)(2,1)S(1)} collective-permute-done((bf16[1,192,768]{2,1,0:T(8,128)(2,1)S(1)}, bf16[1,192,768]{2,1,0:T(8,128)(2,1)S(1)}, u32[]{:S(2)}, u32[]{:S(2)}) %collective-permute-start.41) | collective-permute-done | bytes 294944 | tf_op jit(solution)/shard_map/ppermute | solution.py:46
  345.4 3.2 collective-permute-start.37
  349.5 16.1 %collective-permute-done.42 = bf16[192,768]{1,0:T(8,128)(2,1)S(1)} collective-permute-done((bf16[192,768]{1,0:T(8,128)(2,1)S(1)}, bf16[192,768]{1,0:T(8,128)(2,1)S(1)}, u32[]{:S(2)}, u32[]{:S(2)}) %collective-permute-start.42) | collective-permute-done | bytes 294944 | tf_op jit(solution)/shard_map/ppermute | solution.py:46
  365.6 2.0 collective-permute-start.61
  369.2 3.2 collective-permute-start.46
  375.1 3.1 collective-permute-start.49
  380.9 2.6 collective-permute-start.52
  387.2 3.0 collective-permute-done.53
  393.5 1.6 collective-permute-start.51
  400.5 1.6 maximum_convert_fusion.1
  402.1 1.7 maximum_convert_fusion
  (464 shorter events, 94.0 us)
Async XLA Ops:
  3.8 42.9 %collective-permute-start.4 = (bf16[192,2304]{1,0:T(8,128)(2,1)S(1)}, bf16[192,2304]{1,0:T(8,128)(2,1)}, u32[]{:S(2)}, u32[]{:S(2)}) collective-permute-start(bf16[192,2304]{1,0:T(8,128)(2,1)S(1)} %constant_dynamic-update-slice_fusion.refs_0_), channel_id=1, source_target_pairs={{0,1},{1,0},{2,3},{3,2},{4,5},{5,4},{6,7},{7,6},{8,9},{9,8},{10,11... | collective-permute-start | bytes 2654216 | tf_op jit(solution)/shard_map/ppermute | solution.py:46
  4.4 13.4 %collective-permute-start = (bf16[96,2304]{1,0:T(8,128)(2,1)S(1)}, bf16[96,2304]{1,0:T(8,128)(2,1)S(1)}, u32[]{:S(2)}, u32[]{:S(2)}) collective-permute-start(bf16[96,2304]{1,0:T(8,128)(2,1)S(1)} %constant_dynamic-slice_fusion.10), channel_id=1, source_target_pairs={{0,2},{1,3},{2,0},{3,1},{4,6},{5,7},{6,4},{7,5},{8,10},{9,11},{10,... | collective-permute-start | bytes 1327112 | tf_op jit(solution)/shard_map/ppermute | solution.py:46
  7.0 55.5 %collective-permute-start.7 = (bf16[192,768]{1,0:T(8,128)(2,1)}, bf16[192,768]{1,0:T(8,128)(2,1)}, u32[]{:S(2)}, u32[]{:S(2)}) collective-permute-start(bf16[192,768]{1,0:T(8,128)(2,1)} %refs_0_.1), channel_id=1, source_target_pairs={{0,1},{1,0},{2,3},{3,2},{4,5},{5,4},{6,7},{7,6},{8,9},{9,8},{10,11... | collective-permute-start | bytes 884744 | tf_op jit(solution)/shard_map/ppermute | solution.py:46
  17.8 19.3 %collective-permute-start.1 = (bf16[1,512,768]{2,1,0:T(8,128)(2,1)S(1)}, bf16[1,512,768]{2,1,0:T(8,128)(2,1)S(1)}, u32[]{:S(2)}, u32[]{:S(2)}) collective-permute-start(bf16[1,512,768]{2,1,0:T(8,128)(2,1)S(1)} %bitcast.237), channel_id=1, source_target_pairs={{0,2},{1,3},{2,0},{3,1},{4,6},{5,7},{6,4},{7,5},{8,10},{9,11},{10,... | collective-permute-start | bytes 2359304 | tf_op jit(solution)/shard_map/ppermute | solution.py:46
  19.6 11.5 %collective-permute-start.2 = (bf16[96,2304]{1,0:T(8,128)(2,1)S(1)}, bf16[96,2304]{1,0:T(8,128)(2,1)S(1)}, u32[]{:S(2)}, u32[]{:S(2)}) collective-permute-start(bf16[96,2304]{1,0:T(8,128)(2,1)S(1)} %collective-permute-done.refs_2_), channel_id=1, source_target_pairs={{0,4},{4,0},{8,12},{12,8},{16,20},{20,16},{24,28},{28,24},{1,5},{5... | collective-permute-start | bytes 1327112 | tf_op jit(solution)/shard_map/ppermute | solution.py:46
  38.6 12.9 %collective-permute-start.3 = (bf16[2,512,768]{2,1,0:T(8,128)(2,1)}, bf16[2,512,768]{2,1,0:T(8,128)(2,1)}, u32[]{:S(2)}, u32[]{:S(2)}) collective-permute-start(bf16[2,512,768]{2,1,0:T(8,128)(2,1)} %pad_maximum_fusion.3), channel_id=1, source_target_pairs={{0,1},{1,0},{2,3},{3,2},{4,5},{5,4},{6,7},{7,6},{8,9},{9,8},{10,11... | collective-permute-start | bytes 4718600 | tf_op jit(solution)/shard_map/ppermute | solution.py:46
  45.7 2.1 collective-permute-start.6
  46.8 15.8 %collective-permute-start.8 = (bf16[192,3072]{1,0:T(8,128)(2,1)S(1)}, bf16[192,3072]{1,0:T(8,128)(2,1)S(1)}, u32[]{:S(2)}, u32[]{:S(2)}) collective-permute-start(bf16[192,3072]{1,0:T(8,128)(2,1)S(1)} %copy-done.8), channel_id=1, source_target_pairs={{0,1},{1,0},{2,3},{3,2},{4,5},{5,4},{6,7},{7,6},{8,9},{9,8},{10,11... | collective-permute-start | bytes 3538952 | tf_op jit(solution)/shard_map/ppermute | solution.py:46
  47.2 15.4 %collective-permute-start.9 = (bf16[768,768]{1,0:T(8,128)(2,1)S(1)}, bf16[768,768]{1,0:T(8,128)(2,1)S(1)}, u32[]{:S(2)}, u32[]{:S(2)}) collective-permute-start(bf16[768,768]{1,0:T(8,128)(2,1)S(1)} %copy-done.9), channel_id=1, source_target_pairs={{0,1},{1,0},{2,3},{3,2},{4,5},{5,4},{6,7},{7,6},{8,9},{9,8},{10,11... | collective-permute-start | bytes 3538952 | tf_op jit(solution)/shard_map/ppermute | solution.py:46
  47.8 21.7 %collective-permute-start.10 = (bf16[96,3072]{1,0:T(8,128)(2,1)}, bf16[96,3072]{1,0:T(8,128)(2,1)}, u32[]{:S(2)}, u32[]{:S(2)}) collective-permute-start(bf16[96,3072]{1,0:T(8,128)(2,1)} %constant_dynamic-slice_fusion.9), channel_id=1, source_target_pairs={{0,2},{1,3},{2,0},{3,1},{4,6},{5,7},{6,4},{7,5},{8,10},{9,11},{10,... | collective-permute-start | bytes 1769480 | tf_op jit(solution)/shard_map/ppermute | solution.py:46
  51.5 18.4 %collective-permute-start.11 = (bf16[192,768]{1,0:T(8,128)(2,1)}, bf16[192,768]{1,0:T(8,128)(2,1)S(1)}, u32[]{:S(2)}, u32[]{:S(2)}) collective-permute-start(bf16[192,768]{1,0:T(8,128)(2,1)} %refs_0_.1), channel_id=1, source_target_pairs={{0,2},{1,3},{2,0},{3,1},{4,6},{5,7},{6,4},{7,5},{8,10},{9,11},{10,... | collective-permute-start | bytes 884744 | tf_op jit(solution)/shard_map/ppermute | solution.py:46
  69.9 32.9 %collective-permute-start.12 = (bf16[192,768]{1,0:T(8,128)(2,1)S(1)}, bf16[192,768]{1,0:T(8,128)(2,1)S(1)}, u32[]{:S(2)}, u32[]{:S(2)}) collective-permute-start(bf16[192,768]{1,0:T(8,128)(2,1)S(1)} %collective-permute-done.11.refs_2_), channel_id=1, source_target_pairs={{0,1},{1,0},{2,3},{3,2},{4,5},{5,4},{6,7},{7,6},{8,9},{9,8},{10,11... | collective-permute-start | bytes 884744 | tf_op jit(solution)/shard_map/ppermute | solution.py:46
  80.3 25.4 %collective-permute-start.14 = (bf16[96,3072]{1,0:T(8,128)(2,1)}, bf16[96,3072]{1,0:T(8,128)(2,1)S(1)}, u32[]{:S(2)}, u32[]{:S(2)}) collective-permute-start(bf16[96,3072]{1,0:T(8,128)(2,1)} %collective-permute-done.10.refs_2_), channel_id=1, source_target_pairs={{0,4},{4,0},{8,12},{12,8},{16,20},{20,16},{24,28},{28,24},{1,5},{5... | collective-permute-start | bytes 1769480 | tf_op jit(solution)/shard_map/ppermute | solution.py:46
  81.9 33.7 %collective-permute-start.13 = (bf16[96,3072]{1,0:T(8,128)(2,1)}, bf16[96,3072]{1,0:T(8,128)(2,1)S(1)}, u32[]{:S(2)}, u32[]{:S(2)}) collective-permute-start(bf16[96,3072]{1,0:T(8,128)(2,1)} %collective-permute-done.10.refs_2_), channel_id=1, source_target_pairs={{0,1},{1,0},{2,3},{3,2},{4,5},{5,4},{6,7},{7,6},{8,9},{9,8},{10,11... | collective-permute-start | bytes 1769480 | tf_op jit(solution)/shard_map/ppermute | solution.py:46
  85.6 29.6 %collective-permute-start.16 = (bf16[384,768]{1,0:T(8,128)(2,1)S(1)}, bf16[384,768]{1,0:T(8,128)(2,1)S(1)}, u32[]{:S(2)}, u32[]{:S(2)}) collective-permute-start(bf16[384,768]{1,0:T(8,128)(2,1)S(1)} %copy-done.84), channel_id=1, source_target_pairs={{0,2},{1,3},{2,0},{3,1},{4,6},{5,7},{6,4},{7,5},{8,10},{9,11},{10,... | collective-permute-start | bytes 1769480 | tf_op jit(solution)/shard_map/ppermute | solution.py:46
  105.8 9.8 %collective-permute-start.15 = (bf16[96,3072]{1,0:T(8,128)(2,1)S(1)}, bf16[96,3072]{1,0:T(8,128)(2,1)S(1)}, u32[]{:S(2)}, u32[]{:S(2)}) collective-permute-start(bf16[96,3072]{1,0:T(8,128)(2,1)S(1)} %collective-permute-done.14.refs_4_), channel_id=1, source_target_pairs={{0,1},{1,0},{2,3},{3,2},{4,5},{5,4},{6,7},{7,6},{8,9},{9,8},{10,11... | collective-permute-start | bytes 1769480 | tf_op jit(solution)/shard_map/ppermute | solution.py:46
  115.2 14.7 %collective-permute-start.18 = (bf16[384,768]{1,0:T(8,128)(2,1)S(1)}, bf16[384,768]{1,0:T(8,128)(2,1)S(1)}, u32[]{:S(2)}, u32[]{:S(2)}) collective-permute-start(bf16[384,768]{1,0:T(8,128)(2,1)S(1)} %collective-permute-done.16.refs_2_), channel_id=1, source_target_pairs={{0,4},{4,0},{8,12},{12,8},{16,20},{20,16},{24,28},{28,24},{1,5},{5... | collective-permute-start | bytes 1769480 | tf_op jit(solution)/shard_map/ppermute | solution.py:46
  121.9 13.0 %collective-permute-start.17 = (bf16[384,768]{1,0:T(8,128)(2,1)S(1)}, bf16[384,768]{1,0:T(8,128)(2,1)S(1)}, u32[]{:S(2)}, u32[]{:S(2)}) collective-permute-start(bf16[384,768]{1,0:T(8,128)(2,1)S(1)} %collective-permute-done.16.refs_2_), channel_id=1, source_target_pairs={{0,1},{1,0},{2,3},{3,2},{4,5},{5,4},{6,7},{7,6},{8,9},{9,8},{10,11... | collective-permute-start | bytes 1769480 | tf_op jit(solution)/shard_map/ppermute | solution.py:46
  129.9 5.0 %collective-permute-start.19 = (bf16[384,768]{1,0:T(8,128)(2,1)S(1)}, bf16[384,768]{1,0:T(8,128)(2,1)S(1)}, u32[]{:S(2)}, u32[]{:S(2)}) collective-permute-start(bf16[384,768]{1,0:T(8,128)(2,1)S(1)} %collective-permute-done.18.refs_4_), channel_id=1, source_target_pairs={{0,1},{1,0},{2,3},{3,2},{4,5},{5,4},{6,7},{7,6},{8,9},{9,8},{10,11... | collective-permute-start | bytes 1769480 | tf_op jit(solution)/shard_map/ppermute | solution.py:46
  133.1 23.1 %collective-permute-start.20 = (bf16[1536,768]{1,0:T(8,128)(2,1)}, bf16[1536,768]{1,0:T(8,128)(2,1)}, u32[]{:S(2)}, u32[]{:S(2)}) collective-permute-start(bf16[1536,768]{1,0:T(8,128)(2,1)} %convolution_convert_fusion.1), channel_id=1, source_target_pairs={{0,1},{1,0},{2,3},{3,2},{4,5},{5,4},{6,7},{7,6},{8,9},{9,8},{10,11... | collective-permute-start | bytes 7077896 | tf_op jit(solution)/shard_map/ppermute | solution.py:46
  147.4 16.2 %collective-permute-start.21 = (bf16[384,3072]{1,0:T(8,128)(2,1)}, bf16[384,3072]{1,0:T(8,128)(2,1)}, u32[]{:S(2)}, u32[]{:S(2)}) collective-permute-start(bf16[384,3072]{1,0:T(8,128)(2,1)} %convolution_convert_fusion), channel_id=1, source_target_pairs={{0,1},{1,0},{2,3},{3,2},{4,5},{5,4},{6,7},{7,6},{8,9},{9,8},{10,11... | collective-permute-start | bytes 7077896 | tf_op jit(solution)/shard_map/ppermute | solution.py:46
  160.6 47.6 %collective-permute-start.23 = (bf16[1,768,768]{2,1,0:T(8,128)(2,1)}, bf16[1,768,768]{2,1,0:T(8,128)(2,1)}, u32[]{:S(2)}, u32[]{:S(2)}) collective-permute-start(bf16[1,768,768]{2,1,0:T(8,128)(2,1)} %dynamic-slice_bitcast_fusion), channel_id=1, source_target_pairs={{0,2},{1,3},{2,0},{3,1},{4,6},{5,7},{6,4},{7,5},{8,10},{9,11},{10,... | collective-permute-start | bytes 3538952 | tf_op jit(solution)/shard_map/ppermute | solution.py:46
  167.4 47.6 %collective-permute-start.22 = (bf16[2,96,3072]{2,1,0:T(8,128)(2,1)}, bf16[2,96,3072]{2,1,0:T(8,128)(2,1)}, u32[]{:S(2)}, u32[]{:S(2)}) collective-permute-start(bf16[2,96,3072]{2,1,0:T(8,128)(2,1)} %constant_dynamic-slice_fusion.3), channel_id=1, source_target_pairs={{0,4},{4,0},{8,12},{12,8},{16,20},{20,16},{24,28},{28,24},{1,5},{5... | collective-permute-start | bytes 3538952 | tf_op jit(solution)/shard_map/ppermute | solution.py:46
  175.1 36.5 %collective-permute-start.25 = (bf16[1,512,768]{2,1,0:T(8,128)(2,1)}, bf16[1,512,768]{2,1,0:T(8,128)(2,1)}, u32[]{:S(2)}, u32[]{:S(2)}) collective-permute-start(bf16[1,512,768]{2,1,0:T(8,128)(2,1)} %bitcast.44), channel_id=1, source_target_pairs={{2,0},{3,1},{6,4},{7,5},{10,8},{11,9},{14,12},{15,13},{18,16},{19,... | collective-permute-start | bytes 2359304 | tf_op jit(solution)/shard_map/ppermute | solution.py:62
  178.1 30.1 %collective-permute-start.24 = (bf16[384,768]{1,0:T(8,128)(2,1)}, bf16[384,768]{1,0:T(8,128)(2,1)}, u32[]{:S(2)}, u32[]{:S(2)}) collective-permute-start(bf16[384,768]{1,0:T(8,128)(2,1)} %convolution_convert_fusion.6), channel_id=1, source_target_pairs={{0,1},{1,0},{2,3},{3,2},{4,5},{5,4},{6,7},{7,6},{8,9},{9,8},{10,11... | collective-permute-start | bytes 1769480 | tf_op jit(solution)/shard_map/ppermute | solution.py:46
  188.2 19.9 %collective-permute-start.29 = (f32[1,6,8,512]{3,2,1,0:T(8,128)S(1)}, f32[1,6,8,512]{3,2,1,0:T(8,128)S(1)}, u32[]{:S(2)}, u32[]{:S(2)}) collective-permute-start(f32[1,6,8,512]{3,2,1,0:T(8,128)S(1)} %add_bitcast_fusion.1), channel_id=1, source_target_pairs={{2,0},{3,1},{6,4},{7,5},{10,8},{11,9},{14,12},{15,13},{18,16},{19,... | collective-permute-start | bytes 294920 | tf_op jit(solution)/shard_map/ppermute | solution.py:62
  208.1 20.6 %collective-permute-start.30 = (f32[2,6,8,512]{3,2,1,0:T(8,128)S(1)}, f32[2,6,8,512]{3,2,1,0:T(8,128)}, u32[]{:S(2)}, u32[]{:S(2)}) collective-permute-start(f32[2,6,8,512]{3,2,1,0:T(8,128)S(1)} %pad_maximum_fusion.18), channel_id=1, source_target_pairs={{0,1},{1,0},{2,3},{3,2},{4,5},{5,4},{6,7},{7,6},{8,9},{9,8},{10,11... | collective-permute-start | bytes 589832 | tf_op jit(solution)/shard_map/ppermute | solution.py:62
  209.9 25.2 %collective-permute-start.27 = (bf16[384,768]{1,0:T(8,128)(2,1)S(1)}, bf16[384,768]{1,0:T(8,128)(2,1)}, u32[]{:S(2)}, u32[]{:S(2)}) collective-permute-start(bf16[384,768]{1,0:T(8,128)(2,1)S(1)} %dynamic-slice_bitcast_fusion.1), channel_id=1, source_target_pairs={{0,4},{4,0},{8,12},{12,8},{16,20},{20,16},{24,28},{28,24},{1,5},{5... | collective-permute-start | bytes 1769480 | tf_op jit(solution)/shard_map/ppermute | solution.py:46
  214.5 29.5 %collective-permute-start.26 = (bf16[2,512,768]{2,1,0:T(8,128)(2,1)}, bf16[2,512,768]{2,1,0:T(8,128)(2,1)}, u32[]{:S(2)}, u32[]{:S(2)}) collective-permute-start(bf16[2,512,768]{2,1,0:T(8,128)(2,1)} %pad_maximum_fusion.5), channel_id=1, source_target_pairs={{0,1},{1,0},{2,3},{3,2},{4,5},{5,4},{6,7},{7,6},{8,9},{9,8},{10,11... | collective-permute-start | bytes 4718600 | tf_op jit(solution)/shard_map/ppermute | solution.py:62
  218.5 17.8 %collective-permute-start.28 = (bf16[1,96,3072]{2,1,0:T(8,128)(2,1)}, bf16[1,96,3072]{2,1,0:T(8,128)(2,1)}, u32[]{:S(2)}, u32[]{:S(2)}) collective-permute-start(bf16[1,96,3072]{2,1,0:T(8,128)(2,1)} %constant_dynamic-slice_fusion.2), channel_id=1, source_target_pairs={{0,2},{1,3},{2,0},{3,1},{4,6},{5,7},{6,4},{7,5},{8,10},{9,11},{10,... | collective-permute-start | bytes 1769480 | tf_op jit(solution)/shard_map/ppermute | solution.py:46
  228.8 31.3 %collective-permute-start.31 = (bf16[384,768]{1,0:T(8,128)(2,1)}, bf16[384,768]{1,0:T(8,128)(2,1)}, u32[]{:S(2)}, u32[]{:S(2)}) collective-permute-start(bf16[384,768]{1,0:T(8,128)(2,1)} %convolution_convert_fusion.5), channel_id=1, source_target_pairs={{0,1},{1,0},{2,3},{3,2},{4,5},{5,4},{6,7},{7,6},{8,9},{9,8},{10,11... | collective-permute-start | bytes 1769480 | tf_op jit(solution)/shard_map/ppermute | solution.py:46
  239.6 23.2 %collective-permute-start.34 = (bf16[192,768]{1,0:T(8,128)(2,1)}, bf16[192,768]{1,0:T(8,128)(2,1)}, u32[]{:S(2)}, u32[]{:S(2)}) collective-permute-start(bf16[192,768]{1,0:T(8,128)(2,1)} %get-tuple-element.224), channel_id=1, source_target_pairs={{0,24},{4,28},{8,16},{12,20},{16,8},{20,12},{24,0},{28,4},{1,25},{... | collective-permute-start | bytes 884744 | tf_op jit(solution)/shard_map/ppermute | solution.py:46
  239.6 23.2 %collective-permute-start.33 = (bf16[192,768]{1,0:T(8,128)(2,1)}, bf16[192,768]{1,0:T(8,128)(2,1)}, u32[]{:S(2)}, u32[]{:S(2)}) collective-permute-start(bf16[192,768]{1,0:T(8,128)(2,1)} %get-tuple-element.225), channel_id=1, source_target_pairs={{0,16},{4,20},{8,24},{12,28},{16,0},{20,4},{24,8},{28,12},{1,17},{... | collective-permute-start | bytes 884744 | tf_op jit(solution)/shard_map/ppermute | solution.py:46
  239.6 24.6 %collective-permute-start.32 = (bf16[192,768]{1,0:T(8,128)(2,1)}, bf16[192,768]{1,0:T(8,128)(2,1)}, u32[]{:S(2)}, u32[]{:S(2)}) collective-permute-start(bf16[192,768]{1,0:T(8,128)(2,1)} %get-tuple-element.223), channel_id=1, source_target_pairs={{0,8},{4,12},{8,0},{12,4},{16,24},{20,28},{24,16},{28,20},{1,9},{5... | collective-permute-start | bytes 884744 | tf_op jit(solution)/shard_map/ppermute | solution.py:46
  281.8 31.6 %collective-permute-start.35 = (bf16[1,384,768]{2,1,0:T(8,128)(2,1)}, bf16[1,384,768]{2,1,0:T(8,128)(2,1)}, u32[]{:S(2)}, u32[]{:S(2)}) collective-permute-start(bf16[1,384,768]{2,1,0:T(8,128)(2,1)} %fusion.36), channel_id=1, source_target_pairs={{0,2},{1,3},{2,0},{3,1},{4,6},{5,7},{6,4},{7,5},{8,10},{9,11},{10,... | collective-permute-start | bytes 1769480 | tf_op jit(solution)/shard_map/ppermute | solution.py:46
  283.8 42.5 %collective-permute-start.38 = (bf16[384,768]{1,0:T(8,128)(2,1)}, bf16[384,768]{1,0:T(8,128)(2,1)}, u32[]{:S(2)}, u32[]{:S(2)}) collective-permute-start(bf16[384,768]{1,0:T(8,128)(2,1)} %convolution_convert_fusion.4), channel_id=1, source_target_pairs={{0,1},{1,0},{2,3},{3,2},{4,5},{5,4},{6,7},{7,6},{8,9},{9,8},{10,11... | collective-permute-start | bytes 1769480 | tf_op jit(solution)/shard_map/ppermute | solution.py:46
  283.8 12.2 %collective-permute-start.57 = (bf16[192,768]{1,0:T(8,128)(2,1)}, bf16[192,768]{1,0:T(8,128)(2,1)}, u32[]{:S(2)}, u32[]{:S(2)}) collective-permute-start(bf16[192,768]{1,0:T(8,128)(2,1)} %fusion.42), channel_id=1, source_target_pairs={{0,24},{4,28},{8,16},{12,20},{16,8},{20,12},{24,0},{28,4},{1,25},{... | collective-permute-start | bytes 884744 | tf_op jit(solution)/shard_map/ppermute | solution.py:46
  285.0 27.0 %collective-permute-start.58 = (bf16[192,768]{1,0:T(8,128)(2,1)}, bf16[192,768]{1,0:T(8,128)(2,1)}, u32[]{:S(2)}, u32[]{:S(2)}) collective-permute-start(bf16[192,768]{1,0:T(8,128)(2,1)} %fusion.42), channel_id=1, source_target_pairs={{0,16},{4,20},{8,24},{12,28},{16,0},{20,4},{24,8},{28,12},{1,17},{... | collective-permute-start | bytes 884744 | tf_op jit(solution)/shard_map/ppermute | solution.py:46
  285.3 26.7 %collective-permute-start.56 = (bf16[192,768]{1,0:T(8,128)(2,1)}, bf16[192,768]{1,0:T(8,128)(2,1)}, u32[]{:S(2)}, u32[]{:S(2)}) collective-permute-start(bf16[192,768]{1,0:T(8,128)(2,1)} %fusion.42), channel_id=1, source_target_pairs={{0,8},{4,12},{8,0},{12,4},{16,24},{20,28},{24,16},{28,20},{1,9},{5... | collective-permute-start | bytes 884744 | tf_op jit(solution)/shard_map/ppermute | solution.py:46
  296.0 33.6 %collective-permute-start.40 = (bf16[384,768]{1,0:T(8,128)(2,1)}, bf16[384,768]{1,0:T(8,128)(2,1)S(1)}, u32[]{:S(2)}, u32[]{:S(2)}) collective-permute-start(bf16[384,768]{1,0:T(8,128)(2,1)} %convolution_convert_fusion.3), channel_id=1, source_target_pairs={{0,1},{1,0},{2,3},{3,2},{4,5},{5,4},{6,7},{7,6},{8,9},{9,8},{10,11... | collective-permute-start | bytes 1769480 | tf_op jit(solution)/shard_map/ppermute | solution.py:46
  312.0 33.5 %collective-permute-start.60 = (f32[12,768]{1,0:T(8,128)}, f32[12,768]{1,0:T(8,128)S(1)}, u32[]{:S(2)}, u32[]{:S(2)}) collective-permute-start(f32[12,768]{1,0:T(8,128)} %concatenate.147), channel_id=1, source_target_pairs={{0,1},{1,0},{2,3},{3,2},{4,5},{5,4},{6,7},{7,6},{8,9},{9,8},{10,11... | collective-permute-start | bytes 110600 | tf_op jit(solution)/shard_map/ppermute | solution.py:46
  314.6 19.6 %collective-permute-start.36 = (bf16[192,768]{1,0:T(8,128)(2,1)S(1)}, bf16[192,768]{1,0:T(8,128)(2,1)S(1)}, u32[]{:S(2)}, u32[]{:S(2)}) collective-permute-start(bf16[192,768]{1,0:T(8,128)(2,1)S(1)} %dynamic-slice_bitcast_fusion.4), channel_id=1, source_target_pairs={{0,4},{4,0},{8,12},{12,8},{16,20},{20,16},{24,28},{28,24},{1,5},{5... | collective-permute-start | bytes 884744 | tf_op jit(solution)/shard_map/ppermute | solution.py:46
  327.5 9.9 %collective-permute-start.39 = (bf16[1,192,768]{2,1,0:T(8,128)(2,1)S(1)}, bf16[1,192,768]{2,1,0:T(8,128)(2,1)S(1)}, u32[]{:S(2)}, u32[]{:S(2)}) collective-permute-start(bf16[1,192,768]{2,1,0:T(8,128)(2,1)S(1)} %dynamic-slice_bitcast_fusion.3), channel_id=1, source_target_pairs={{0,2},{1,3},{2,0},{3,1},{4,6},{5,7},{6,4},{7,5},{8,10},{9,11},{10,... | collective-permute-start | bytes 884744 | tf_op jit(solution)/shard_map/ppermute | solution.py:46
  329.8 13.6 %collective-permute-start.41 = (bf16[1,192,768]{2,1,0:T(8,128)(2,1)S(1)}, bf16[1,192,768]{2,1,0:T(8,128)(2,1)S(1)}, u32[]{:S(2)}, u32[]{:S(2)}) collective-permute-start(bf16[1,192,768]{2,1,0:T(8,128)(2,1)S(1)} %dynamic-slice_bitcast_fusion.2), channel_id=1, source_target_pairs={{0,2},{1,3},{2,0},{3,1},{4,6},{5,7},{6,4},{7,5},{8,10},{9,11},{10,... | collective-permute-start | bytes 884744 | tf_op jit(solution)/shard_map/ppermute | solution.py:46
  329.9 70.2 %collective-permute-start.59 = (bf16[768,768]{1,0:T(8,128)(2,1)S(1)}, bf16[768,768]{1,0:T(8,128)(2,1)S(1)}, u32[]{:S(2)}, u32[]{:S(2)}) collective-permute-start(bf16[768,768]{1,0:T(8,128)(2,1)S(1)} %pad_maximum_fusion.6), channel_id=1, source_target_pairs={{0,4},{4,0},{8,12},{12,8},{16,20},{20,16},{24,28},{28,24},{1,5},{5... | collective-permute-start | bytes 3538952 | tf_op jit(solution)/shard_map/ppermute | solution.py:46
  343.7 21.9 %collective-permute-start.42 = (bf16[192,768]{1,0:T(8,128)(2,1)S(1)}, bf16[192,768]{1,0:T(8,128)(2,1)S(1)}, u32[]{:S(2)}, u32[]{:S(2)}) collective-permute-start(bf16[192,768]{1,0:T(8,128)(2,1)S(1)} %fusion.55), channel_id=1, source_target_pairs={{0,4},{4,0},{8,12},{12,8},{16,20},{20,16},{24,28},{28,24},{1,5},{5... | collective-permute-start | bytes 884744 | tf_op jit(solution)/shard_map/ppermute | solution.py:46
  344.2 23.7 %collective-permute-start.44 = (bf16[48,768]{1,0:T(8,128)(2,1)S(1)}, bf16[48,768]{1,0:T(8,128)(2,1)S(1)}, u32[]{:S(2)}, u32[]{:S(2)}) collective-permute-start(bf16[48,768]{1,0:T(8,128)(2,1)S(1)} %get-tuple-element.269), channel_id=1, source_target_pairs={{0,24},{4,28},{8,16},{12,20},{16,8},{20,12},{24,0},{28,4},{1,25},{... | collective-permute-start | bytes 221192 | tf_op jit(solution)/shard_map/ppermute | solution.py:46
  345.4 22.5 %collective-permute-start.43 = (bf16[48,768]{1,0:T(8,128)(2,1)S(1)}, bf16[48,768]{1,0:T(8,128)(2,1)S(1)}, u32[]{:S(2)}, u32[]{:S(2)}) collective-permute-start(bf16[48,768]{1,0:T(8,128)(2,1)S(1)} %get-tuple-element.270), channel_id=1, source_target_pairs={{0,16},{4,20},{8,24},{12,28},{16,0},{20,4},{24,8},{28,12},{1,17},{... | collective-permute-start | bytes 221192 | tf_op jit(solution)/shard_map/ppermute | solution.py:46
  345.4 22.5 %collective-permute-start.37 = (bf16[48,768]{1,0:T(8,128)(2,1)S(1)}, bf16[48,768]{1,0:T(8,128)(2,1)S(1)}, u32[]{:S(2)}, u32[]{:S(2)}) collective-permute-start(bf16[48,768]{1,0:T(8,128)(2,1)S(1)} %get-tuple-element.268), channel_id=1, source_target_pairs={{0,8},{4,12},{8,0},{12,4},{16,24},{20,28},{24,16},{28,20},{1,9},{5... | collective-permute-start | bytes 221192 | tf_op jit(solution)/shard_map/ppermute | solution.py:46
  365.6 6.9 %collective-permute-start.61 = (f32[12,768]{1,0:T(8,128)S(1)}, f32[12,768]{1,0:T(8,128)S(1)}, u32[]{:S(2)}, u32[]{:S(2)}) collective-permute-start(f32[12,768]{1,0:T(8,128)S(1)} %add.409), channel_id=1, source_target_pairs={{0,2},{1,3},{2,0},{3,1},{4,6},{5,7},{6,4},{7,5},{8,10},{9,11},{10,... | collective-permute-start | bytes 110600 | tf_op jit(solution)/shard_map/ppermute | solution.py:46
  368.0 7.1 %collective-permute-start.48 = (bf16[48,768]{1,0:T(8,128)(2,1)S(1)}, bf16[48,768]{1,0:T(8,128)(2,1)S(1)}, u32[]{:S(2)}, u32[]{:S(2)}) collective-permute-start(bf16[48,768]{1,0:T(8,128)(2,1)S(1)} %get-tuple-element.266), channel_id=1, source_target_pairs={{0,24},{4,28},{8,16},{12,20},{16,8},{20,12},{24,0},{28,4},{1,25},{... | collective-permute-start | bytes 221192 | tf_op jit(solution)/shard_map/ppermute | solution.py:46
  369.2 10.1 %collective-permute-start.47 = (bf16[48,768]{1,0:T(8,128)(2,1)S(1)}, bf16[48,768]{1,0:T(8,128)(2,1)S(1)}, u32[]{:S(2)}, u32[]{:S(2)}) collective-permute-start(bf16[48,768]{1,0:T(8,128)(2,1)S(1)} %get-tuple-element.267), channel_id=1, source_target_pairs={{0,16},{4,20},{8,24},{12,28},{16,0},{20,4},{24,8},{28,12},{1,17},{... | collective-permute-start | bytes 221192 | tf_op jit(solution)/shard_map/ppermute | solution.py:46
  369.2 10.1 %collective-permute-start.46 = (bf16[48,768]{1,0:T(8,128)(2,1)S(1)}, bf16[48,768]{1,0:T(8,128)(2,1)S(1)}, u32[]{:S(2)}, u32[]{:S(2)}) collective-permute-start(bf16[48,768]{1,0:T(8,128)(2,1)S(1)} %get-tuple-element.265), channel_id=1, source_target_pairs={{0,8},{4,12},{8,0},{12,4},{16,24},{20,28},{24,16},{28,20},{1,9},{5... | collective-permute-start | bytes 221192 | tf_op jit(solution)/shard_map/ppermute | solution.py:46
  372.5 8.4 %collective-permute-start.45 = (bf16[48,768]{1,0:T(8,128)(2,1)S(1)}, bf16[48,768]{1,0:T(8,128)(2,1)S(1)}, u32[]{:S(2)}, u32[]{:S(2)}) collective-permute-start(bf16[48,768]{1,0:T(8,128)(2,1)S(1)} %fusion.62), channel_id=1, source_target_pairs={{0,24},{4,28},{8,16},{12,20},{16,8},{20,12},{24,0},{28,4},{1,25},{... | collective-permute-start | bytes 221192 | tf_op jit(solution)/shard_map/ppermute | solution.py:46
  375.1 8.4 %collective-permute-start.49 = (bf16[48,768]{1,0:T(8,128)(2,1)S(1)}, bf16[48,768]{1,0:T(8,128)(2,1)S(1)}, u32[]{:S(2)}, u32[]{:S(2)}) collective-permute-start(bf16[48,768]{1,0:T(8,128)(2,1)S(1)} %fusion.62), channel_id=1, source_target_pairs={{0,16},{4,20},{8,24},{12,28},{16,0},{20,4},{24,8},{28,12},{1,17},{... | collective-permute-start | bytes 221192 | tf_op jit(solution)/shard_map/ppermute | solution.py:46
  379.3 5.2 %collective-permute-start.50 = (bf16[48,768]{1,0:T(8,128)(2,1)S(1)}, bf16[48,768]{1,0:T(8,128)(2,1)S(1)}, u32[]{:S(2)}, u32[]{:S(2)}) collective-permute-start(bf16[48,768]{1,0:T(8,128)(2,1)S(1)} %fusion.62), channel_id=1, source_target_pairs={{0,8},{4,12},{8,0},{12,4},{16,24},{20,28},{24,16},{28,20},{1,9},{5... | collective-permute-start | bytes 221192 | tf_op jit(solution)/shard_map/ppermute | solution.py:46
  379.3 6.3 %collective-permute-start.62 = (f32[12,768]{1,0:T(8,128)S(1)}, f32[12,768]{1,0:T(8,128)S(1)}, u32[]{:S(2)}, u32[]{:S(2)}) collective-permute-start(f32[12,768]{1,0:T(8,128)S(1)} %add.410), channel_id=1, source_target_pairs={{0,4},{4,0},{8,12},{12,8},{16,20},{20,16},{24,28},{28,24},{1,5},{5... | collective-permute-start | bytes 110600 | tf_op jit(solution)/shard_map/ppermute | solution.py:46
  380.9 6.3 %collective-permute-start.52 = (bf16[48,768]{1,0:T(8,128)(2,1)S(1)}, bf16[48,768]{1,0:T(8,128)(2,1)S(1)}, u32[]{:S(2)}, u32[]{:S(2)}) collective-permute-start(bf16[48,768]{1,0:T(8,128)(2,1)S(1)} %fusion.59), channel_id=1, source_target_pairs={{0,24},{4,28},{8,16},{12,20},{16,8},{20,12},{24,0},{28,4},{1,25},{... | collective-permute-start | bytes 221192 | tf_op jit(solution)/shard_map/ppermute | solution.py:46
  383.5 6.7 %collective-permute-start.53 = (bf16[48,768]{1,0:T(8,128)(2,1)S(1)}, bf16[48,768]{1,0:T(8,128)(2,1)S(1)}, u32[]{:S(2)}, u32[]{:S(2)}) collective-permute-start(bf16[48,768]{1,0:T(8,128)(2,1)S(1)} %fusion.59), channel_id=1, source_target_pairs={{0,16},{4,20},{8,24},{12,28},{16,0},{20,4},{24,8},{28,12},{1,17},{... | collective-permute-start | bytes 221192 | tf_op jit(solution)/shard_map/ppermute | solution.py:46
  384.5 5.7 %collective-permute-start.54 = (bf16[48,768]{1,0:T(8,128)(2,1)S(1)}, bf16[48,768]{1,0:T(8,128)(2,1)S(1)}, u32[]{:S(2)}, u32[]{:S(2)}) collective-permute-start(bf16[48,768]{1,0:T(8,128)(2,1)S(1)} %fusion.59), channel_id=1, source_target_pairs={{0,8},{4,12},{8,0},{12,4},{16,24},{20,28},{24,16},{28,20},{1,9},{5... | collective-permute-start | bytes 221192 | tf_op jit(solution)/shard_map/ppermute | solution.py:46
  385.7 6.0 %collective-permute-start.63 = (f32[12,768]{1,0:T(8,128)S(1)}, f32[12,768]{1,0:T(8,128)S(1)}, u32[]{:S(2)}, u32[]{:S(2)}) collective-permute-start(f32[12,768]{1,0:T(8,128)S(1)} %add.411), channel_id=1, source_target_pairs={{0,8},{4,12},{8,0},{12,4},{16,24},{20,28},{24,16},{28,20},{1,9},{5... | collective-permute-start | bytes 110600 | tf_op jit(solution)/shard_map/ppermute | solution.py:46
  391.6 5.3 %collective-permute-start.64 = (f32[12,768]{1,0:T(8,128)S(1)}, f32[12,768]{1,0:T(8,128)S(1)}, u32[]{:S(2)}, u32[]{:S(2)}) collective-permute-start(f32[12,768]{1,0:T(8,128)S(1)} %add.412), channel_id=1, source_target_pairs={{0,16},{4,20},{8,24},{12,28},{16,0},{20,4},{24,8},{28,12},{1,17},{... | collective-permute-start | bytes 110600 | tf_op jit(solution)/shard_map/ppermute | solution.py:46
  393.5 10.3 %collective-permute-start.51 = (bf16[192,768]{1,0:T(8,128)(2,1)}, bf16[192,768]{1,0:T(8,128)(2,1)}, u32[]{:S(2)}, u32[]{:S(2)}) collective-permute-start(bf16[192,768]{1,0:T(8,128)(2,1)} %pad_maximum_fusion.16), channel_id=1, source_target_pairs={{0,4},{4,0},{8,12},{12,8},{16,20},{20,16},{24,28},{28,24},{1,5},{5... | collective-permute-start | bytes 884744 | tf_op jit(solution)/shard_map/ppermute | solution.py:46
  395.1 12.2 %collective-permute-start.55 = (bf16[192,768]{1,0:T(8,128)(2,1)}, bf16[192,768]{1,0:T(8,128)(2,1)}, u32[]{:S(2)}, u32[]{:S(2)}) collective-permute-start(bf16[192,768]{1,0:T(8,128)(2,1)} %pad_maximum_fusion.17), channel_id=1, source_target_pairs={{0,4},{4,0},{8,12},{12,8},{16,20},{20,16},{24,28},{28,24},{1,5},{5... | collective-permute-start | bytes 884744 | tf_op jit(solution)/shard_map/ppermute | solution.py:46
  (107 other events, 912.1 us)
